TPU v7x, 32 devices: a whole 2x2x4 slice. The times are simulated.
32 devices in a mesh: ctx: 2 (over core), seq: 16 (over z, y, x).
Axes of the slice: x: 2, y: 2, z: 4, core: 2. Of those that a mesh axis runs over, the one named last changes fastest.
Arguments:
- hidden: bfloat16 [2, 2048, 1024], P('ctx', 'seq'), may hold values from -6 to 6
- out_grad: bfloat16 [2, 2048, 1024], P('ctx', 'seq'), may hold values from -6 to 6
- resets: int32 [2, 2048], P('ctx', 'seq'), may hold values from 0 to 1, as said below
- valid: int32 [2], P('ctx'), may hold values from 256 to 2048, as said below
- norm_gain: bfloat16 [1024], P('seq'), may hold values from 0.099609375 to 1.8984375
- in_weight: bfloat16 [1024, 4096], P('seq'), may hold values from -0.1875 to 0.1875
- conv_weight: bfloat16 [2048, 4], P('seq'), may hold values from -0.5 to 0.5
- conv_bias: bfloat16 [2048], P('seq'), may hold values from -0.5 to 0.5
- x_weight: bfloat16 [2048, 96], P('seq'), may hold values from -0.125 to 0.125
- dt_weight: bfloat16 [2048, 64], P('seq'), may hold values from -0.75 to 0.75
- dt_bias: bfloat16 [2048], P('seq'), may hold values from -5 to -3
- a_log: bfloat16 [2048, 16], P('seq'), may hold values from -17 to 3
- skip_gain: bfloat16 [2048], P('seq'), may hold values from 0.5 to 1.5
- out_weight: bfloat16 [2048, 1024], P('seq'), may hold values from -0.0625 to 0.0625
Outputs:
- out: bfloat16 [2, 2048, 1024], P('ctx', 'seq')
- grad_hidden: float32 [2, 2048, 1024], P('ctx', 'seq')
- grad_norm_gain: float32 [1024], P('seq')
- grad_in_weight: float32 [1024, 4096], P('seq')
- grad_conv_weight: float32 [2048, 4], P('seq')
- grad_conv_bias: float32 [2048], P('seq')
- grad_x_weight: float32 [2048, 96], P('seq')
- grad_dt_weight: float32 [2048, 64], P('seq')
- grad_dt_bias: float32 [2048], P('seq')
- grad_a_log: float32 [2048, 16], P('seq')
- grad_skip_gain: float32 [2048], P('seq')
- grad_out_weight: float32 [2048, 1024], P('seq')
Inputs may be any that keep to these rules, and one draw needn't show every extreme that they name: Tokens t >= valid[c] of context c are padding; one context, drawn from the seed, is full. `resets`: 1 marks the first token of a cluster. In the full context one cluster starts within the first 128 tokens and ends within the last 128.
All inputs are finite; a program needn't handle non-finite values.
Results may differ from a plain program's by a relative error of at most 0.0081.
Values may be sent and summed in bfloat16 or wider, within the bound.
A program may use at most 448 MiB of HBM per device.

v0:
```python
import jax
import jax.numpy as jnp
from jax import lax
from jax.sharding import PartitionSpec as P

epsilon = 1e-05
highest = lax.Precision.HIGHEST
contract_last = (((1,), (1,)), ((), ()))
contract_first = (((0,), (0,)), ((), ()))


def passed_along(block, axis, distance):
    devices = range(lax.axis_size(axis))
    route = [(i - distance, i) for i in devices if i - distance in devices]
    return lax.ppermute(block, axis, route)


def entering_2(part, axis, combine, identity, reverse):
    count = lax.axis_size(axis)
    place = lax.axis_index(axis)
    ahead = count - 1 - place if reverse else place
    gathered = jax.tree.map(lambda a: lax.all_gather(a, axis), part)
    state = jax.tree.map(lambda a, e: jnp.zeros_like(a) + jnp.asarray(e, a.dtype), part, identity)

    def one(hop, state):
        source = count - 1 - hop if reverse else hop
        return combine(
            state, jax.tree.map(lambda a: lax.dynamic_index_in_dim(a, source, 0, False), gathered)
        )

    return lax.fori_loop(0, ahead, one, state)


def silu_slope(value):
    sigma = jax.nn.sigmoid(value)
    return sigma * (1.0 + value * (1.0 - sigma))


def combine_pair(earlier, later):
    return (earlier[0] * later[0], later[0] * earlier[1] + later[1])


def decays_of(delta_blk, keep_blk, a_matrix):
    return keep_blk[:, None, None] * jnp.exp(delta_blk[:, :, None] * a_matrix[None])


def shards(
    hidden,
    out_grad,
    resets,
    valid,
    norm_gain,
    in_weight,
    conv_weight,
    conv_bias,
    x_weight,
    dt_weight,
    dt_bias,
    a_log,
    skip_gain,
    out_weight,
):
    gathered = (
        lax.all_gather(norm_gain, "seq", axis=0, tiled=True),
        lax.all_gather(in_weight, "seq", axis=0, tiled=True),
        lax.all_gather(conv_weight, "seq", axis=0, tiled=True),
        lax.all_gather(conv_bias, "seq", axis=0, tiled=True),
        lax.all_gather(x_weight, "seq", axis=0, tiled=True),
        lax.all_gather(dt_weight, "seq", axis=0, tiled=True),
        lax.all_gather(dt_bias, "seq", axis=0, tiled=True),
        lax.all_gather(a_log, "seq", axis=0, tiled=True),
        lax.all_gather(skip_gain, "seq", axis=0, tiled=True),
        lax.all_gather(out_weight, "seq", axis=0, tiled=True),
    )
    gain_full, w_in, w_conv, b_conv, w_x, w_dt, b_dt, a_logs, w_skip, w_out = gathered
    tokens = hidden.shape[1]
    inner = w_out.shape[0]
    rank = w_dt.shape[1]
    state = a_logs.shape[1]
    taps = w_conv.shape[1]
    places = lax.axis_index("seq") * tokens + jnp.arange(tokens, dtype=jnp.int32)
    live_mask = (places < valid[0]).astype(jnp.float32)
    reset_f = resets[0].astype(jnp.float32)
    keep_mask = 1.0 - reset_f
    source = hidden[0].astype(jnp.float32)
    rscale = lax.rsqrt(jnp.mean(source * source, axis=-1, keepdims=True) + epsilon)
    scaled = source * rscale
    gain_f = gain_full.astype(jnp.float32)
    normed = (scaled * gain_f).astype(jnp.bfloat16)
    projected = jnp.dot(normed, w_in, preferred_element_type=jnp.float32)
    x_part = projected[:, :inner].astype(jnp.bfloat16)
    z_part = projected[:, inner:]
    rim_rows = passed_along(x_part[tokens - (taps - 1) :], "seq", 1)
    extended = jnp.concatenate([rim_rows, x_part], 0).astype(jnp.float32)
    conv_taps = w_conv.astype(jnp.float32)
    conv_out = b_conv.astype(jnp.float32) + sum(
        (conv_taps[:, offset] * extended[offset : offset + tokens] for offset in range(taps))
    )
    signal_low = jax.nn.silu(conv_out).astype(jnp.bfloat16)
    signal = signal_low.astype(jnp.float32)
    x_dbl = jnp.dot(signal_low, w_x, preferred_element_type=jnp.float32)
    dt_low = x_dbl[:, :rank].astype(jnp.bfloat16)
    b_input = x_dbl[:, rank : rank + state]
    c_output = x_dbl[:, rank + state :]
    dt_pre = lax.dot_general(
        dt_low, w_dt, contract_last, preferred_element_type=jnp.float32
    ) + b_dt.astype(jnp.float32)
    delta = jax.nn.softplus(dt_pre)
    a_matrix = -jnp.exp(a_logs.astype(jnp.float32))
    drive = delta * signal
    reset_count = jnp.cumsum(reset_f)
    reset_before = reset_count - reset_f
    delta_sum = jnp.cumsum(delta, 0)
    delta_before = delta_sum - delta
    reset_total = reset_count[-1]
    delta_total = delta_sum[-1]
    alive_upto = (reset_count == 0.0).astype(jnp.float32)
    alive_before = (reset_before == 0.0).astype(jnp.float32)
    alive_after = (reset_total - reset_count == 0.0).astype(jnp.float32)
    span_len = min(64, tokens)
    n_blocks = tokens // span_len
    roll_by = min(16, span_len)

    def split_blocks(value):
        return value.reshape((n_blocks, span_len) + value.shape[1:])

    delta_b = split_blocks(delta)
    drive_b = split_blocks(drive)
    binput_b = split_blocks(b_input)
    coutput_b = split_blocks(c_output)
    keep_b = split_blocks(keep_mask)
    dsum_b = split_blocks(delta_sum)
    upto_b = split_blocks(alive_upto)
    after_b = split_blocks(alive_after)
    ones_state = jnp.ones((inner, state), jnp.float32)
    zero_state = jnp.zeros((inner, state), jnp.float32)
    group_prod = (reset_total == 0.0).astype(jnp.float32) * jnp.exp(delta_total[:, None] * a_matrix)

    def forward_step(state_now, blk):
        delta_blk, drive_blk, binput_blk, coutput_blk, keep_blk = blk
        decays = decays_of(delta_blk, keep_blk, a_matrix)

        def token_step(state_tok, item):
            decay_now, drive_now, binput_now, coutput_now = item
            state_next = decay_now * state_tok + drive_now[:, None] * binput_now[None, :]
            return (state_next, jnp.sum(state_next * coutput_now[None, :], -1))

        state_end, outputs = lax.scan(
            token_step, state_now, (decays, drive_blk, binput_blk, coutput_blk), unroll=roll_by
        )
        return (state_end, (state_now, outputs))

    group_state, (local_starts, scan_local) = lax.scan(
        forward_step, zero_state, (delta_b, drive_b, binput_b, coutput_b, keep_b)
    )
    entering = entering_2(
        (group_prod, group_state), "seq", combine_pair, (ones_state, zero_state), False
    )
    state_in = entering[1]

    def lift_block(blk):
        dsum_blk, upto_blk, coutput_blk = blk
        lifted = (
            upto_blk[:, None, None]
            * jnp.exp(dsum_blk[:, :, None] * a_matrix[None])
            * state_in[None]
        )
        return jnp.sum(lifted * coutput_blk[:, None, :], -1)

    lifted_out = lax.map(lift_block, (dsum_b, upto_b, coutput_b))
    scanned = (scan_local + lifted_out).reshape(tokens, inner) + w_skip.astype(jnp.float32) * signal
    gate_act = jax.nn.silu(z_part)
    mixed = (scanned * gate_act).astype(jnp.bfloat16)
    branch = jnp.dot(mixed, w_out, preferred_element_type=jnp.float32)
    result = (source + live_mask[:, None] * branch).astype(jnp.bfloat16)
    regathered = (
        lax.all_gather(norm_gain, "seq", axis=0, tiled=True),
        lax.all_gather(in_weight, "seq", axis=0, tiled=True),
        lax.all_gather(conv_weight, "seq", axis=0, tiled=True),
        lax.all_gather(conv_bias, "seq", axis=0, tiled=True),
        lax.all_gather(x_weight, "seq", axis=0, tiled=True),
        lax.all_gather(dt_weight, "seq", axis=0, tiled=True),
        lax.all_gather(dt_bias, "seq", axis=0, tiled=True),
        lax.all_gather(a_log, "seq", axis=0, tiled=True),
        lax.all_gather(skip_gain, "seq", axis=0, tiled=True),
        lax.all_gather(out_weight, "seq", axis=0, tiled=True),
    )
    gain_full, w_in, w_conv, b_conv, w_x, w_dt, b_dt, a_logs, w_skip, w_out = regathered
    gain_f = gain_full.astype(jnp.float32)
    conv_taps = w_conv.astype(jnp.float32)
    a_matrix = -jnp.exp(a_logs.astype(jnp.float32))
    cotangent = out_grad[0].astype(jnp.float32)
    g_branch = (live_mask[:, None] * cotangent).astype(jnp.bfloat16)
    g_mixed = lax.dot_general(g_branch, w_out, contract_last, preferred_element_type=jnp.float32)
    g_scan = g_mixed * gate_act
    g_zpart = g_mixed * scanned * silu_slope(z_part)
    g_skip_full = jnp.sum(g_scan * signal, 0)
    gscan_b = split_blocks(g_scan)

    def push_block(total, blk):
        dsum_blk, upto_blk, coutput_blk, gscan_blk = blk
        weight_blk = upto_blk[:, None, None] * jnp.exp(dsum_blk[:, :, None] * a_matrix[None])
        return (
            total + jnp.sum(weight_blk * gscan_blk[:, :, None] * coutput_blk[:, None, :], 0),
            None,
        )

    passed_local, _ = lax.scan(push_block, zero_state, (dsum_b, upto_b, coutput_b, gscan_b))
    leaving = entering_2(
        (group_prod, passed_local), "seq", combine_pair, (ones_state, zero_state), True
    )
    passed_in = leaving[1]
    start_rows = jnp.arange(n_blocks) * span_len
    start_alive = alive_before[start_rows]
    start_delta = delta_before[start_rows]
    block_starts = (
        local_starts
        + start_alive[:, None, None]
        * jnp.exp(start_delta[:, :, None] * a_matrix[None])
        * state_in[None]
    )

    def backward_step(carried, blk):
        passed, grad_amat = carried
        (
            start_state,
            delta_blk,
            drive_blk,
            binput_blk,
            coutput_blk,
            gscan_blk,
            keep_blk,
            dsum_blk,
            after_blk,
        ) = blk
        decays = decays_of(delta_blk, keep_blk, a_matrix)

        def ahead_step(state_tok, item):
            decay_now, drive_now, binput_now = item
            state_next = decay_now * state_tok + drive_now[:, None] * binput_now[None, :]
            return (state_next, state_next)

        _, states_blk = lax.scan(
            ahead_step, start_state, (decays, drive_blk, binput_blk), unroll=roll_by
        )
        before = jnp.concatenate([start_state[None], states_blk[:-1]], 0)

        def behind_step(passed_tok, item):
            decay_now, coutput_now, gscan_now = item
            adjoint = gscan_now[:, None] * coutput_now[None, :] + passed_tok
            return (decay_now * adjoint, adjoint)

        passed, adjoints_local = lax.scan(
            behind_step, passed, (decays, coutput_blk, gscan_blk), reverse=True, unroll=roll_by
        )
        reach = after_blk[:, None, None] * jnp.exp(
            (delta_total[None] - dsum_blk)[:, :, None] * a_matrix[None]
        )
        adjoints = adjoints_local + reach * passed_in[None]
        flow = adjoints * before * decays
        g_delta_decay = jnp.sum(flow * a_matrix[None], -1)
        grad_amat = grad_amat + jnp.sum(flow * delta_blk[:, :, None], 0)
        g_drive = jnp.einsum("qen,qn->qe", adjoints, binput_blk, precision=highest)
        g_binput = jnp.einsum("qen,qe->qn", adjoints, drive_blk, precision=highest)
        g_coutput = jnp.einsum("qen,qe->qn", states_blk, gscan_blk, precision=highest)
        return ((passed, grad_amat), (g_delta_decay, g_drive, g_binput, g_coutput))

    (_, grad_amat), pieces = lax.scan(
        backward_step,
        (zero_state, zero_state),
        (block_starts, delta_b, drive_b, binput_b, coutput_b, gscan_b, keep_b, dsum_b, after_b),
        reverse=True,
    )
    g_delta_decay = pieces[0].reshape(tokens, inner)
    g_drive = pieces[1].reshape(tokens, inner)
    g_binput = pieces[2].reshape(tokens, state)
    g_coutput = pieces[3].reshape(tokens, state)
    g_delta = g_delta_decay + g_drive * signal
    g_pre = (g_delta * jax.nn.sigmoid(dt_pre)).astype(jnp.bfloat16)
    g_dtlow = jnp.dot(g_pre, w_dt, preferred_element_type=jnp.float32)
    g_xdbl = jnp.concatenate([g_dtlow, g_binput, g_coutput], 1).astype(jnp.bfloat16)
    g_signal = (
        g_scan * w_skip.astype(jnp.float32)
        + g_drive * delta
        + lax.dot_general(g_xdbl, w_x, contract_last, preferred_element_type=jnp.float32)
    )
    g_conv = g_signal * silu_slope(conv_out)
    g_extended = sum(
        (
            jnp.pad(conv_taps[:, offset] * g_conv, ((offset, taps - 1 - offset), (0, 0)))
            for offset in range(taps)
        )
    )
    returned = passed_along(g_extended[: taps - 1], "seq", -1)
    g_xpart = g_extended[taps - 1 :] + jnp.pad(returned, ((tokens - (taps - 1), 0), (0, 0)))
    g_proj = jnp.concatenate([g_xpart, g_zpart], 1).astype(jnp.bfloat16)
    g_normed = lax.dot_general(g_proj, w_in, contract_last, preferred_element_type=jnp.float32)
    g_hat = g_normed * gain_f
    grad_source = (
        rscale * g_hat
        - source * rscale * rscale * rscale * jnp.mean(g_hat * source, axis=-1, keepdims=True)
        + cotangent
    )
    g_gain = jnp.sum(g_normed * scaled, 0)
    g_wconv = jnp.stack(
        [jnp.sum(g_conv * extended[offset : offset + tokens], 0) for offset in range(taps)], 1
    )
    g_bconv = jnp.sum(g_conv, 0)
    g_bdt = jnp.sum(g_pre.astype(jnp.float32), 0)
    g_alog = grad_amat * a_matrix
    weight_rows = lax.dot_general(
        normed, g_proj, contract_first, preferred_element_type=jnp.float32
    )
    g_win_rows, g_gain_rows = lax.psum_scatter(
        (weight_rows, g_gain), "seq", scatter_dimension=0, tiled=True
    )
    xw_rows = lax.dot_general(
        signal_low, g_xdbl, contract_first, preferred_element_type=jnp.float32
    )
    dtw_rows = lax.dot_general(g_pre, dt_low, contract_first, preferred_element_type=jnp.float32)
    outw_rows = lax.dot_general(mixed, g_branch, contract_first, preferred_element_type=jnp.float32)
    (
        g_wconv_rows,
        g_bconv_rows,
        g_wx_rows,
        g_wdt_rows,
        g_bdt_rows,
        g_alog_rows,
        g_skip_rows,
        g_wout_rows,
    ) = lax.psum_scatter(
        (g_wconv, g_bconv, xw_rows, dtw_rows, g_bdt, g_alog, g_skip_full, outw_rows),
        "seq",
        scatter_dimension=0,
        tiled=True,
    )
    totals = lax.psum(
        (
            g_gain_rows,
            g_win_rows,
            g_wconv_rows,
            g_bconv_rows,
            g_wx_rows,
            g_wdt_rows,
            g_bdt_rows,
            g_alog_rows,
            g_skip_rows,
            g_wout_rows,
        ),
        "ctx",
    )
    return (
        result[None],
        grad_source[None],
        totals[0],
        totals[1],
        totals[2],
        totals[3],
        totals[4],
        totals[5],
        totals[6],
        totals[7],
        totals[8],
        totals[9],
    )


def solution(mesh):
    return jax.shard_map(
        shards,
        mesh=mesh,
        in_specs=(
            P("ctx", "seq", None),
            P("ctx", "seq", None),
            P("ctx", "seq"),
            P("ctx"),
            P("seq"),
            P("seq", None),
            P("seq", None),
            P("seq"),
            P("seq", None),
            P("seq", None),
            P("seq"),
            P("seq", None),
            P("seq"),
            P("seq", None),
        ),
        out_specs=(
            P("ctx", "seq", None),
            P("ctx", "seq", None),
            P("seq"),
            P("seq", None),
            P("seq", None),
            P("seq"),
            P("seq", None),
            P("seq", None),
            P("seq"),
            P("seq", None),
            P("seq"),
            P("seq", None),
        ),
        check_vma=False,
    )
```

profile of v0, /device:TPU:0, one launch (start us, length us, event | category | flops | bytes accessed | tf_op | source)
XLA Modules:
  0.0 1955.8 jit_solution(13781849616002549358)
XLA Ops:
  11.6 44.2 %all-reduce.5 = bf16[1024]{0:T(1024)(128)(2,1)S(1)} all-reduce(bf16[1024]{0:T(1024)(128)(2,1)S(1)} %dynamic-update-slice), channel_id=1, replica_groups=mesh['ctx'=2,'seq'=16] {'seq'}, use_global_device_ids=true, to_apply=%add.5 | all-reduce | flops 1024 | bytes 4096
  56.4 36.2 %all_gather.59 = bf16[2048,4]{0,1:T(4,128)(2,1)S(1)} all-gather(bf16[128,4]{0,1:T(4,128)(2,1)} %param.38), channel_id=1, replica_groups=mesh['ctx'=2,'seq'=16] {'seq'}, dimensions={0}, use_global_device_ids=true | all-gather | bytes 17408 | tf_op jit(solution)/shard_map/all_gather | solution.py:66
  92.6 41.5 %all_gather.63 = bf16[2048,64]{0,1:T(8,128)(2,1)S(1)} all-gather(bf16[128,64]{0,1:T(8,128)(2,1)} %param.41), channel_id=1, replica_groups=mesh['ctx'=2,'seq'=16] {'seq'}, dimensions={0}, use_global_device_ids=true | all-gather | bytes 278528 | tf_op jit(solution)/shard_map/all_gather | solution.py:69
  135.3 41.0 %all_gather.62 = bf16[2048,96]{0,1:T(8,128)(2,1)} all-gather(bf16[128,96]{0,1:T(8,128)(2,1)} %param.40), channel_id=1, replica_groups=mesh['ctx'=2,'seq'=16] {'seq'}, dimensions={0}, use_global_device_ids=true | all-gather | bytes 417792 | tf_op jit(solution)/shard_map/all_gather | solution.py:68
  177.1 6.2 fusion.243
  183.4 3.9 collective-permute-start
  187.3 36.7 %all_gather.65 = bf16[2048,16]{0,1:T(8,128)(2,1)S(1)} all-gather(bf16[128,16]{0,1:T(8,128)(2,1)S(1)} %copy-done.62), channel_id=1, replica_groups=mesh['ctx'=2,'seq'=16] {'seq'}, dimensions={0}, use_global_device_ids=true | all-gather | bytes 69632 | tf_op jit(solution)/shard_map/all_gather | solution.py:71
  224.0 37.1 %all-gather.4 = bf16[16,1,128]{2,1,0:T(2,128)(2,1)S(1)} all-gather(bf16[1,1,128]{2,1,0:T(2,128)(2,1)S(1)} %bitcast.1341), channel_id=1, replica_groups=mesh['ctx'=2,'seq'=16] {'seq'}, dimensions={0}, use_global_device_ids=true | all-gather | bytes 4352 | tf_op jit(solution)/shard_map/all_gather | solution.py:70
  261.1 35.5 %all-gather.3 = bf16[16,1,128]{2,1,0:T(2,128)(2,1)S(1)} all-gather(bf16[1,1,128]{2,1,0:T(2,128)(2,1)S(1)} %bitcast.1342), channel_id=1, replica_groups=mesh['ctx'=2,'seq'=16] {'seq'}, dimensions={0}, use_global_device_ids=true | all-gather | bytes 4352 | tf_op jit(solution)/shard_map/all_gather | solution.py:67
  299.3 7.9 fusion.179
  316.7 3.2 fusion.213
  320.0 9.1 while.169
  331.3 70.5 %while.165 = (s32[]{:T(128)}, f32[2048,16]{0,1:T(8,128)S(1)}, f32[2,2048,16]{1,2,0:T(8,128)}, f32[2,64,2048]{2,1,0:T(8,128)}, f32[2,64]{1,0:T(2,128)}, /*index=5...) while((s32[]{:T(128)}, f32[2048,16]{0,1:T(8,128)S(1)}, ...), condition=%wide.region_20.21_spmd, body=%wide.region_1.20_spmd.sunk | while | flops 7569427 | bytes 19522424 | solution.py:153
  334.0 4.7 exponential_multiply_fusion.5
  339.4 26.3 %while.173 = (s32[]{:T(128)}, f32[2048,16]{0,1:T(8,128)S(1)}, f32[4,16,2048]{2,1,0:T(8,128)S(1)}, f32[4,16,2048,16]{2,3,1,0:T(8,128)}, f32[4,16,2048]{2,1,0:T(8,...) while((s32[]{:T(128)}, f32[2048,16]{0,1:T(8,128)S(1)}, ...), condition=%wide.region_19.19_spmd, body=%wide.region_2.18_spmd.sunk | while | flops 3375121 | bytes 7019645 | solution.py:148
  369.3 4.7 exponential_multiply_fusion.5
  374.8 26.2 %while.173 = (s32[]{:T(128)}, f32[2048,16]{0,1:T(8,128)S(1)}, f32[4,16,2048]{2,1,0:T(8,128)S(1)}, f32[4,16,2048,16]{2,3,1,0:T(8,128)}, f32[4,16,2048]{2,1,0:T(8,...) while((s32[]{:T(128)}, f32[2048,16]{0,1:T(8,128)S(1)}, ...), condition=%wide.region_19.19_spmd, body=%wide.region_2.18_spmd.sunk | while | flops 3375121 | bytes 7019645 | solution.py:148
  402.7 37.2 %all-gather.5 = bf16[16,1,128]{2,1,0:T(2,128)(2,1)S(1)} all-gather(bf16[1,1,128]{2,1,0:T(2,128)(2,1)S(1)} %bitcast.1343), channel_id=1, replica_groups=mesh['ctx'=2,'seq'=16] {'seq'}, dimensions={0}, use_global_device_ids=true | all-gather | bytes 4352 | tf_op jit(solution)/shard_map/all_gather | solution.py:72
  443.0 3.1 copy.118
  446.1 4.1 copy.105
  450.9 45.1 %while.168 = (s32[]{:T(128)}, f32[2048,16]{0,1:T(8,128)}, s32[]{:T(128)}, f32[16,2048,16]{1,2,0:T(8,128)}, f32[16,2048,16]{1,0,2:T(8,128)}, /*index=5*/s32[]{:T(128)}, s32[]{:T(128)}, s32[]{:T(128)}, s32[]{:T(128)}) while((s32[]{:T(128)}, f32[2048,16]{0,1:T(8,128)}, s32[]{:T(128)}, f32[16,2048,16]{1,2,0:T(8,128)}, ...), condition=%wide.region_32.33_spmd, body=%wide.region_31.32_spmd.sunk | while | flops 65542 | bytes 786587 | solution.py:31
  496.0 4.2 copy.104
  504.5 435.9 %while.172 = (s32[]{:T(128)}, f32[2048,16]{0,1:T(8,128)S(1)}, f32[2048,16]{0,1:T(8,128)}, f32[2,64,2048]{2,1,0:T(8,128)}, f32[2,64,2048]{2,1,0:T(8,128)}, /*inde...) while((s32[]{:T(128)}, f32[2048,16]{0,1:T(8,128)S(1)}, ...), condition=%wide.region_40.41_spmd.clone, body=%wide.region_33.40_spmd.clone.sunk | while | flops 126648352 | bytes 277412928 | solution.py:268
  523.1 4.7 exponential_multiply_fusion.6
  529.2 4.3 broadcast.279.clone
  533.5 51.8 %while.174 = (s32[]{:T(128)}, f32[2048,16]{0,1:T(8,128)S(1)}, f32[4,16,2048,16]{2,3,1,0:T(8,128)}, f32[4,16,2048,16]{2,3,1,0:T(8,128)}, f32[4,16,2048]{2,1,0:T(8...) while((s32[]{:T(128)}, f32[2048,16]{0,1:T(8,128)S(1)}, ...), condition=%wide.region_35.35_spmd, body=%wide.region_34.34_spmd.sunk | while | flops 2490385 | bytes 13197537 | solution.py:253
  588.7 4.3 broadcast.279.clone.1
  593.0 77.3 %while.175 = (s32[]{:T(128)}, f32[2048,16]{0,1:T(8,128)S(1)}, f32[4,16,2048,16]{2,3,1,0:T(8,128)}, f32[4,16,2048,16]{2,3,1,0:T(8,128)}, f32[4,16,2048]{2,1,0:T(8...) while((s32[]{:T(128)}, f32[2048,16]{0,1:T(8,128)S(1)}, ...), condition=%wide.region_37.37_spmd, body=%wide.region_36.36_spmd.sunk | while | flops 2359312 | bytes 13056229 | solution.py:243
  670.3 4.0 slice.983
  674.3 4.2 pad_maximum_fusion.9
  682.5 12.4 multiply_reduce_fusion.35
  696.4 4.7 bitcast_add_fusion.2
  701.1 4.7 fusion.304
  707.4 9.5 fusion.306
  718.1 11.8 fusion.308
  732.5 4.7 exponential_multiply_fusion.6
  738.6 4.3 broadcast.279.clone
  742.8 51.8 %while.174 = (s32[]{:T(128)}, f32[2048,16]{0,1:T(8,128)S(1)}, f32[4,16,2048,16]{2,3,1,0:T(8,128)}, f32[4,16,2048,16]{2,3,1,0:T(8,128)}, f32[4,16,2048]{2,1,0:T(8...) while((s32[]{:T(128)}, f32[2048,16]{0,1:T(8,128)S(1)}, ...), condition=%wide.region_35.35_spmd, body=%wide.region_34.34_spmd.sunk | while | flops 2490385 | bytes 13197537 | solution.py:253
  798.1 4.3 broadcast.279.clone.1
  802.4 77.3 %while.175 = (s32[]{:T(128)}, f32[2048,16]{0,1:T(8,128)S(1)}, f32[4,16,2048,16]{2,3,1,0:T(8,128)}, f32[4,16,2048,16]{2,3,1,0:T(8,128)}, f32[4,16,2048]{2,1,0:T(8...) while((s32[]{:T(128)}, f32[2048,16]{0,1:T(8,128)S(1)}, ...), condition=%wide.region_37.37_spmd, body=%wide.region_36.36_spmd.sunk | while | flops 2359312 | bytes 13056229 | solution.py:243
  879.7 4.0 slice.983
  883.7 4.2 pad_maximum_fusion.9
  891.8 12.4 multiply_reduce_fusion.35
  905.8 4.7 bitcast_add_fusion.2
  910.5 4.7 fusion.304
  916.9 9.5 fusion.306
  927.6 11.8 fusion.308
  941.5 14.2 while.167
  943.2 4.4 multiply_reduce_fusion.33
  950.2 4.4 multiply_reduce_fusion.33
  957.7 4.1 convert_reduce_fusion
  969.8 5.5 fusion.198
  978.4 4.7 collective-permute-done.1
  983.3 8.2 fusion.186
  993.0 6.4 fusion.194
  999.4 105.1 %all-reduce.10 = (f32[1024]{0:T(1024)S(1)}, f32[2048]{0:T(1024)S(1)}, f32[2048]{0:T(1024)S(1)}, f32[2048]{0:T(1024)S(1)}) all-reduce(f32[1024]{0:T(1024)S(1)} %get-tuple-element.1218, f32[2048]{0:T(1024)S(1)} %get-tuple-element.1217, f32[2048]{0:T(1024)S(1)} %get-tuple-element.1420, ...), channel_id=5, replica_groups=mesh['ctx'=2,'seq'=16] {'seq'}, use_global_device_ids=true, to_apply=%region_43.44.clone | all-reduce | flops 7168 | bytes 57344
  1108.3 44.2 %reduce-scatter.15.cloned.1.call-done = f32[128,16]{0,1:T(8,128)} async-done(((f32[2048,16]{0,1:T(8,128)}), f32[128,16]{0,1:T(8,128)}) %reduce-scatter.15.cloned.1.call-update) | async-done | bytes 8208 | tf_op jit(solution)/shard_map/reduce_scatter | solution.py:331
  1152.5 75.7 %reduce-scatter.13.cloned.1.call-done = f32[128,64]{0,1:T(8,128)} async-done(((f32[2048,64]{0,1:T(8,128)}), f32[128,64]{0,1:T(8,128)}) %reduce-scatter.13.cloned.1.call-update) | async-done | bytes 32784 | tf_op jit(solution)/shard_map/reduce_scatter | solution.py:331
  1228.2 124.1 %reduce-scatter.11.cloned.1.call-done = f32[128,96]{0,1:T(8,128)} async-done(((f32[2048,96]{0,1:T(8,128)}), f32[128,96]{0,1:T(8,128)}) %reduce-scatter.11.cloned.1.call-update) | async-done | bytes 49168 | tf_op jit(solution)/shard_map/reduce_scatter | solution.py:331
  1352.4 179.1 %reduce-scatter.17.cloned.1.call-done = f32[128,1024]{1,0:T(8,128)} async-done(((f32[2048,1024]{1,0:T(8,128)}), f32[128,1024]{1,0:T(8,128)}) %reduce-scatter.17.cloned.1.call-update) | async-done | bytes 524304 | tf_op jit(solution)/shard_map/reduce_scatter | solution.py:331
  1531.5 351.2 %reduce-scatter.9.cloned.1.call-done = f32[64,4096]{1,0:T(8,128)} async-done(((f32[1024,4096]{1,0:T(8,128)}), f32[64,4096]{1,0:T(8,128)}) %reduce-scatter.9.cloned.1.call-update) | async-done | bytes 1048592 | tf_op jit(solution)/shard_map/reduce_scatter | solution.py:314
  1882.8 3.6 fusion.174
  1887.4 23.4 %all-reduce.16.cloned.1.call-done = (f32[64]{0:T(128)}, f32[128,4]{0,1:T(4,128)}, f32[128]{0:T(128)}, f32[128,96]{0,1:T(8,128)}, f32[128,64]{0,1:T(8,128)}, /*in...) async-done(((f32[64]{0:T(128)}, f32[128,4]{0,1:T(4,128)}, f32[128]{0:T(128)}, f32[128,96]{0,1:T(8,128)}, f32[128,64]{0,1:T(8,128)}, /*index=5*/f32[128]{0:T(128)}, ...) | async-done | bytes 93968 | tf_op jit(solution)/shard_map/psum | solution.py:337
  1910.9 24.2 %all-reduce.18.cloned.1.call-done = (f32[64,4096]{1,0:T(8,128)}, f32[128,1024]{1,0:T(8,128)}) async-done(((f32[64,4096]{1,0:T(8,128)}, f32[128,1024]{1,0:T(8,128)}), (f32[64,4096]{1,0:T(8,128)}, f32[128,1024]{1,0:T(8,128)})) %all-reduce.18.cloned.1.call-update) | async-done | bytes 1572880 | tf_op jit(solution)/shard_map/psum | solution.py:337
  (815 shorter events, 469.4 us)
Async XLA Ops:
  7.2 169.9 %all-gather.12.cloned.1.call-start = ((), (), s32[]{:S(2)}) async-start(), calls=%async_computation.6 | async-start | bytes 8912896 | tf_op jit(solution)/shard_map/all_gather | solution.py:65
  7.9 291.3 %all-gather.14.cloned.1.call-start = ((), (), s32[]{:S(2)}) async-start(), calls=%async_computation.7 | async-start | bytes 4456448 | tf_op jit(solution)/shard_map/all_gather | solution.py:73
  8.7 434.3 %all-gather.16.cloned.1.call-start = ((), (), s32[]{:S(2)}) async-start(), calls=%async_computation.13 | async-start | bytes 2228224 | tf_op jit(solution)/shard_map/all_gather | solution.py:22
  55.8 127.6 %copy-start.32 = (f32[1024]{0:T(1024)}, f32[1024]{0:T(1024)S(1)}, u32[]{:S(2)}) copy-start(f32[1024]{0:T(1024)S(1)} %convert_element_type.126) | copy-start | bytes 12292
  92.6 206.6 %copy-start.63 = (f32[128]{0:T(128)}, f32[128]{0:T(128)S(1)}, u32[]{:S(2)}) copy-start(f32[128]{0:T(128)S(1)} %compare_convert_fusion.1) | copy-start | bytes 1540
  134.1 173.4 %copy-start.22 = (bf16[2048,64]{0,1:T(8,128)(2,1)}, bf16[2048,64]{0,1:T(8,128)(2,1)S(1)}, u32[]{:S(2)}) copy-start(bf16[2048,64]{0,1:T(8,128)(2,1)S(1)} %all_gather.63) | copy-start | bytes 786436
  176.3 7.0 copy-start.49
  177.0 122.2 %copy-start.52 = (f32[2048,1]{0,1:T(1,128)}, f32[2048,1]{0,1:T(1,128)S(1)}, u32[]{:S(2)}) copy-start(f32[2048,1]{0,1:T(1,128)S(1)} %get-tuple-element.1577) | copy-start | bytes 24580
  177.0 122.2 %copy-start.54 = (f32[2048,1]{0,1:T(1,128)}, f32[2048,1]{0,1:T(1,128)S(1)}, u32[]{:S(2)}) copy-start(f32[2048,1]{0,1:T(1,128)S(1)} %get-tuple-element.1578) | copy-start | bytes 24580
  177.0 122.2 %copy-start.56 = (f32[2048,1]{0,1:T(1,128)}, f32[2048,1]{0,1:T(1,128)S(1)}, u32[]{:S(2)}) copy-start(f32[2048,1]{0,1:T(1,128)S(1)} %get-tuple-element.1579) | copy-start | bytes 24580
  177.0 122.2 %copy-start.58 = (f32[2048,1]{0,1:T(1,128)}, f32[2048,1]{0,1:T(1,128)S(1)}, u32[]{:S(2)}) copy-start(f32[2048,1]{0,1:T(1,128)S(1)} %get-tuple-element.1580) | copy-start | bytes 24580
  177.0 10.2 copy-start.62
  177.0 47.0 %copy-start.67 = (bf16[128]{0:T(256)(128)(2,1)S(1)}, bf16[128]{0:T(256)(128)(2,1)}, u32[]{:S(2)}) copy-start(bf16[128]{0:T(256)(128)(2,1)} %param.42) | copy-start | bytes 772
  177.1 84.0 %copy-start.68 = (bf16[128]{0:T(256)(128)(2,1)S(1)}, bf16[128]{0:T(256)(128)(2,1)}, u32[]{:S(2)}) copy-start(bf16[128]{0:T(256)(128)(2,1)} %param.39) | copy-start | bytes 772
  177.1 122.2 %copy-start.30 = (bf16[1,128,1024]{2,1,0:T(8,128)(2,1)S(1)}, bf16[1,128,1024]{2,1,0:T(8,128)(2,1)}, u32[]{:S(2)}) copy-start(bf16[1,128,1024]{2,1,0:T(8,128)(2,1)} %param.33) | copy-start | bytes 786436
  183.4 114.7 %collective-permute-start = (bf16[3,2048]{1,0:T(4,128)(2,1)S(1)}, bf16[3,2048]{1,0:T(4,128)(2,1)S(1)}, u32[]{:S(2)}, u32[]{:S(2)}) collective-permute-start(bf16[3,2048]{1,0:T(4,128)(2,1)S(1)} %slice.933), channel_id=1, source_target_pairs={{0,1},{1,2},{2,3},{3,4},{4,5},{5,6},{6,7},{7,8},{8,9},{9,10},{10,1... | collective-permute-start | bytes 36872 | tf_op jit(solution)/shard_map/ppermute | solution.py:15
  224.0 87.7 %copy-start.35 = (bf16[2048,16]{0,1:T(8,128)(2,1)}, bf16[2048,16]{0,1:T(8,128)(2,1)S(1)}, u32[]{:S(2)}) copy-start(bf16[2048,16]{0,1:T(8,128)(2,1)S(1)} %all_gather.65) | copy-start | bytes 196612
  299.3 7.9 copy-start.25
  307.2 12.8 copy-start.7
  307.2 5.4 copy-start.70
  307.2 6.0 copy-start.40
  307.5 12.5 copy-start.37
  311.7 8.2 copy-start.27
  312.5 133.6 %all-gather.20.cloned.1.call-start = ((), (), s32[]{:S(2)}) async-start(), calls=%async_computation.15 | async-start | bytes 2228224 | tf_op jit(solution)/shard_map/all_gather | solution.py:22
  329.7 166.3 %all-gather.18.cloned.1.call-start = ((), (), s32[]{:S(2)}) async-start(), calls=%async_computation.14 | async-start | bytes 2228224 | tf_op jit(solution)/shard_map/all_gather | solution.py:22
  331.2 71.3 %copy-start.66 = (f32[128]{0:T(128)S(1)}, f32[128]{0:T(128)}, u32[]{:S(2)}) copy-start(f32[128]{0:T(128)} %get-tuple-element.1221) | copy-start | bytes 1540
  331.3 71.4 %copy-start.69 = (bf16[128]{0:T(256)(128)(2,1)S(1)}, bf16[128]{0:T(256)(128)(2,1)}, u32[]{:S(2)}) copy-start(bf16[128]{0:T(256)(128)(2,1)} %param.44) | copy-start | bytes 772
  331.3 109.2 %copy-start.65 = (f32[128]{0:T(128)S(1)}, f32[128]{0:T(128)}, u32[]{:S(2)}) copy-start(f32[128]{0:T(128)} %get-tuple-element.1220) | copy-start | bytes 1540
  331.3 109.2 %copy-start.71 = (s32[1,128]{1,0:T(1,128)S(1)}, s32[1,128]{1,0:T(1,128)}, u32[]{:S(2)}) copy-start(s32[1,128]{1,0:T(1,128)} %param.34) | copy-start | bytes 1540
  402.5 704.4 %reduce-scatter.19.cloned.1.call-start = ((), (), s32[]{:S(2)}) async-start(), calls=%async_computation.16 | async-start | bytes 1114112
  521.3 160.6 %copy-start.60 = (f32[2,64]{1,0:T(2,128)}, f32[2,64]{1,0:T(2,128)S(1)}, u32[]{:S(2)}) copy-start(f32[2,64]{1,0:T(2,128)S(1)} %get-tuple-element.2934) | copy-start | bytes 1540 | tf_op jit(solution)/shard_map/while
  674.3 5.8 copy-start.1
  696.4 11.0 slice-start
  696.4 11.0 slice-start.1
  718.1 11.9 copy-start.43
  718.1 11.9 copy-start.46
  718.1 12.5 copy-start.61
  730.6 160.6 %copy-start.60 = (f32[2,64]{1,0:T(2,128)}, f32[2,64]{1,0:T(2,128)S(1)}, u32[]{:S(2)}) copy-start(f32[2,64]{1,0:T(2,128)S(1)} %get-tuple-element.2934) | copy-start | bytes 1540 | tf_op jit(solution)/shard_map/while
  883.6 5.8 copy-start.1
  905.8 11.0 slice-start
  905.8 11.0 slice-start.1
  927.5 11.9 copy-start.43
  927.5 11.9 copy-start.46
  927.5 12.5 copy-start.61
  941.5 14.2 copy-start.48
  941.5 14.3 copy-start.45
  941.5 16.0 copy-start.8
  941.5 16.0 copy-start.42
  942.4 5.2 copy-start.17
  949.4 5.2 copy-start.17
  962.2 5.2 copy-start.38
  966.6 185.9 %reduce-scatter.15.cloned.1.call-start = ((), (), s32[]{:S(2)}) async-start(), calls=%async_computation.11 | async-start | bytes 139264 | tf_op jit(solution)/shard_map/reduce_scatter | solution.py:331
  967.4 260.8 %reduce-scatter.13.cloned.1.call-start = ((), (), s32[]{:S(2)}) async-start(), calls=%async_computation.10 | async-start | bytes 557056 | tf_op jit(solution)/shard_map/reduce_scatter | solution.py:331
  968.5 383.8 %reduce-scatter.11.cloned.1.call-start = ((), (), s32[]{:S(2)}) async-start(), calls=%async_computation.9 | async-start | bytes 835584 | tf_op jit(solution)/shard_map/reduce_scatter | solution.py:331
  969.8 561.7 %reduce-scatter.17.cloned.1.call-start = ((), (), s32[]{:S(2)}) async-start(), calls=%async_computation.12 | async-start | bytes 8912896 | tf_op jit(solution)/shard_map/reduce_scatter | solution.py:331
  975.4 907.4 %reduce-scatter.9.cloned.1.call-start = ((), (), s32[]{:S(2)}) async-start(), calls=%async_computation.8 | async-start | bytes 17825792 | tf_op jit(solution)/shard_map/reduce_scatter | solution.py:314
  976.5 6.7 copy-start.9
  976.5 6.7 copy-start.33
  976.6 6.7 copy-start.50
  976.6 6.5 collective-permute-start.1
  991.5 919.4 %all-reduce.16.cloned.1.call-start = ((), (), s32[]{:S(2)}) async-start(), calls=%async_computation.17 | async-start | bytes 188416 | tf_op jit(solution)/shard_map/psum | solution.py:337
  993.0 6.4 copy-start.51
  999.4 887.0 %copy-start.31 = (bf16[1,128,1024]{2,1,0:T(8,128)(2,1)S(1)}, bf16[1,128,1024]{2,1,0:T(8,128)(2,1)}, u32[]{:S(2)}) copy-start(bf16[1,128,1024]{2,1,0:T(8,128)(2,1)} %param.33) | copy-start | bytes 786436
  1352.3 582.7 %all-reduce.18.cloned.1.call-start = ((), (), s32[]{:S(2)}) async-start(), calls=%async_computation.18 | async-start | bytes 3145728 | tf_op jit(solution)/shard_map/psum | solution.py:337
  (45 other events, 145.2 us)
Sparse Core Ops, SparseCore 0:
  10.8 121.7 all-gather.11
  135.4 76.6 all-gather.13
  312.6 58.2 all-gather.15
  373.5 59.3 all-gather.19
  435.5 59.2 all-gather.17
  966.7 110.4 reduce-scatter.18
  1080.1 72.3 reduce-scatter.14
  1155.3 72.8 reduce-scatter.12
  1233.6 118.6 reduce-scatter.10
  1354.6 176.8 reduce-scatter.16
  1533.9 348.7 reduce-scatter.8
  1886.8 24.0 all-reduce.15
  1913.4 21.6 all-reduce.17
where the time goes:
time: 1970 us; the launch traced here: 1960 us
  waiting for transfers between devices  828 us (42%)
  blocking collectives  414 us (21%)
  other arithmetic  390 us (20%)
  local copies, waits for them, and re-layouts  181 us (9%)
  matrix products  97.4 us (5%)
  loops' own time  20 us (1%)
    reduce_scatter x4, waiting for transfers between devices, shards(): lax.psum_scatter((g_wconv, g_bconv, xw_rows, dtw_rows, g_bdt, g_alog, g_s...  423 us
    reduce_scatter x1, waiting for transfers between devices, shards(): lax.psum_scatter((weight_rows, g_gain), 'seq', scatter_dimension=0, tiled...  351 us
    while x186, other arithmetic  196 us
    unnamed x2, blocking collectives  149 us
    psum x2, waiting for transfers between devices, shards(): lax.psum((g_gain_rows, g_win_rows, g_wconv_rows, g_bconv_rows, g_wx_rows,...  47.6 us
    reduce_sum x48, other arithmetic, token_step(): return (state_next, jnp.sum(state_next * coutput_now[None, :], -1))  47.6 us
    all_gather x1, blocking collectives, shards(): lax.all_gather(dt_weight, 'seq', axis=0, tiled=True)  41.5 us
    all_gather x1, blocking collectives, shards(): lax.all_gather(x_weight, 'seq', axis=0, tiled=True)  41 us
  transfers between devices with their start and end apart: 15, of which 8 were waited for; matrix products, arithmetic and copies ran while one was open for 10% of the time, Pallas kernels for 0%

commit v1 on v0

--- a/solution.py
+++ b/solution.py
@@ -1,6 +1,10 @@
+import functools
+
 import jax
 import jax.numpy as jnp
 from jax import lax
+from jax.experimental import pallas as pl
+from jax.experimental.pallas import tpu as pltpu
 from jax.sharding import PartitionSpec as P
 
 epsilon = 1e-05
@@ -365,9 +369,1440 @@
     )
 
 
+MESH = pl.DeviceIdType.MESH
+F32 = jnp.float32
+BF16 = jnp.bfloat16
+ROWS = 128
+GROUPS = 8
+LANES = 128
+WIDE = 512
+LOG2E = 1.4426950408889634
+
+
+def place():
+    seq = lax.axis_index("seq")
+    return lax.axis_index("ctx"), seq, seq // 4, (seq // 2) % 2, seq % 2
+
+
+def chip(z, y, x):
+    return z * 4 + y * 2 + x
+
+
+class Semaphores:
+    def __init__(self, send, receive):
+        self.send, self.receive = send, receive
+        self.sends = self.receives = 0
+
+    def new_send(self):
+        self.sends += 1
+        return self.send.at[self.sends - 1]
+
+    def new_receive(self):
+        self.receives += 1
+        return self.receive.at[self.receives - 1]
+
+    def copy(self, source, target, core, seq, send=None, receive=None):
+        return pltpu.make_async_remote_copy(
+            src_ref=source,
+            dst_ref=target,
+            send_sem=self.new_send() if send is None else send,
+            recv_sem=self.new_receive() if receive is None else receive,
+            device_id=(core, seq),
+            device_id_type=MESH,
+        )
+
+
+def joint(region, copy_sems):
+    c, _, z, y, x = place()
+    send, receive = copy_sems
+    return pltpu.make_async_remote_copy(
+        src_ref=region,
+        dst_ref=region,
+        send_sem=send,
+        recv_sem=receive,
+        device_id=(c, chip(z, y, 1 - x)),
+        device_id_type=MESH,
+    )
+
+
+def partner(z, j):
+    return (z, z + 1 - 2 * (z % 2), (z + 2) % 4, 3 - z)[j]
+
+
+class Gather:
+    slots = 4
+
+    def __init__(self, sems, buf):
+        c, _, z, y, x = place()
+        own = self.slot(0)
+        self.first = [
+            sems.copy(buf.at[:, own, y, x], buf.at[:, own, y, x], c, chip(partner(z, j), y, x))
+            for j in (1, 2, 3)
+        ]
+        send2, send3 = sems.new_send(), sems.new_send()
+        self.second, self.second_all, self.third, self.third_all = [], [], [], []
+        for j in range(self.slots):
+            s = self.slot(j)
+            got = sems.new_receive()
+            self.second.append(
+                [
+                    sems.copy(buf.at[0, s, y, x], buf.at[0, s, y, x], c, chip(z, 1 - y, x), send2, got),
+                    sems.copy(buf.at[1, s, y, x], buf.at[1, s, y, x], c, chip(z, y, 1 - x), send2, got),
+                ]
+            )
+            self.second_all.append(joint(buf.at[:, s, y, x], (send2, got)))
+            got = sems.new_receive()
+            self.third.append(
+                [
+                    sems.copy(buf.at[0, s, :, x], buf.at[0, s, :, x], c, chip(z, y, 1 - x), send3, got),
+                    sems.copy(buf.at[1, s, y], buf.at[1, s, y], c, chip(z, 1 - y, x), send3, got),
+                ]
+            )
+            self.third_all.append(joint(buf.at[:, s, :, x], (send3, got)))
+        self.second_sent = joint(buf.at[:, :, y, x], (send2, got))
+        self.third_sent = joint(buf.at[:, :, :, x], (send3, got))
+
+    def slot(self, j):
+        return partner(place()[2], j)
+
+    def start(self):
+        for copy in self.first:
+            copy.start()
+
+    def arrived(self, j):
+        if j > 0:
+            self.first[j - 1].wait_recv()
+
+    def relay(self, j):
+        self.arrived(j)
+        for copy in self.second[j]:
+            copy.start()
+
+    def cross(self, j):
+        self.second_all[j].wait_recv()
+        for copy in self.third[j]:
+            copy.start()
+
+    def slot_done(self, j):
+        self.third_all[j].wait_recv()
+
+    def done(self):
+        for j in range(self.slots):
+            self.slot_done(j)
+
+    def sent(self):
+        for copy in self.first:
+            copy.wait_send()
+        self.sent_rest()
+
+    def sent_rest(self):
+        self.second_sent.wait_send()
+        self.third_sent.wait_send()
+
+
+def is_active():
+    c, _, z, _, _ = place()
+    return z // 2 == c
+
+
+def is_passive():
+    return jnp.logical_not(is_active())
+
+
+def half_slot(j):
+    z = place()[2]
+    return z % 2 if j == 0 else 1 - z % 2
+
+
+class HalfGather(Gather):
+    slots = 2
+
+    def slot(self, j):
+        return half_slot(j)
+
+    def start(self):
+        @pl.when(is_active())
+        def _():
+            for copy in self.first:
+                copy.start()
+
+    def arrived(self, j):
+        if j == 1:
+
+            @pl.when(is_active())
+            def _():
+                self.first[0].wait_recv()
+
+        @pl.when(is_passive())
+        def _():
+            self.first[1 + j].wait_recv()
+
+    def sent(self):
+        @pl.when(is_active())
+        def _():
+            for copy in self.first:
+                copy.wait_send()
+
+        self.sent_rest()
+
+
+class SmallGather:
+    def __init__(self, sems, buf):
+        c, _, z, y, x = place()
+        s = half_slot(0)
+        self.first = sems.copy(buf.at[s, y, x], buf.at[s, y, x], c, chip(z, y, 1 - x))
+        self.second = sems.copy(buf.at[s, y], buf.at[s, y], c, chip(z, 1 - y, x))
+        self.third = [
+            sems.copy(buf.at[s], buf.at[s], c, chip(partner(z, j), y, x)) for j in (1, 2, 3)
+        ]
+
+    def start(self):
+        @pl.when(is_active())
+        def _():
+            self.first.start()
+
+    def relay(self):
+        @pl.when(is_active())
+        def _():
+            self.first.wait_recv()
+            self.second.start()
+
+    def cross(self):
+        @pl.when(is_active())
+        def _():
+            self.second.wait_recv()
+            for copy in self.third:
+                copy.start()
+
+    def done(self):
+        @pl.when(is_active())
+        def _():
+            self.third[0].wait_recv()
+
+        @pl.when(is_passive())
+        def _():
+            self.third[1].wait_recv()
+            self.third[2].wait_recv()
+
+    def sent(self):
+        @pl.when(is_active())
+        def _():
+            for copy in [self.first, self.second] + self.third:
+                copy.wait_send()
+
+
+def add_into(total, part):
+    total[...] = total[...] + part[...]
+
+
+class Scatter:
+    order = (2, 3, 1, 0)
+
+    def __init__(self, sems, grad, came1, came2, came3):
+        c, _, z, y, x = place()
+        self.grad, self.came1, self.came2, self.came3 = grad, came1, came2, came3
+        send1, send2 = sems.new_send(), sems.new_send()
+        self.first, self.first_all, self.second, self.second_all = [], [], [], []
+        for j in range(len(self.order)):
+            s = self.slot(j)
+            got = sems.new_receive()
+            self.first.append(
+                [
+                    sems.copy(grad.at[0, s, :, 1 - x], came1.at[0, s], c, chip(z, y, 1 - x), send1, got),
+                    sems.copy(grad.at[1, s, 1 - y], came1.at[1, s], c, chip(z, 1 - y, x), send1, got),
+                ]
+            )
+            self.first_all.append(joint(came1.at[:, s], (send1, got)))
+            got = sems.new_receive()
+            self.second.append(
+                [
+                    sems.copy(grad.at[0, s, 1 - y, x], came2.at[0, s], c, chip(z, 1 - y, x), send2, got),
+                    sems.copy(grad.at[1, s, y, 1 - x], came2.at[1, s], c, chip(z, y, 1 - x), send2, got),
+                ]
+            )
+            self.second_all.append(joint(came2.at[:, s], (send2, got)))
+        self.first_sent = joint(came1, (send1, got))
+        self.second_sent = joint(came2, (send2, got))
+        got = sems.new_receive()
+        self.third = [
+            sems.copy(
+                grad.at[:, self.slot(self.third_slot(j)), y, x],
+                came3.at[j - 1],
+                c,
+                chip(partner(z, j), y, x),
+                None,
+                got,
+            )
+            for j in (1, 2, 3)
+        ]
+        self.third_all = joint(came3, (send2, got))
+
+    def slot(self, j):
+        return partner(place()[2], j)
+
+    def third_slot(self, j):
+        return j
+
+    def push1(self, j):
+        for copy in self.first[j]:
+            copy.start()
+
+    def push2(self, j):
+        _, _, _, y, x = place()
+        s = self.slot(j)
+        self.first_all[j].wait_recv()
+        add_into(self.grad.at[0, s, 1 - y, x], self.came1.at[0, s, 1 - y])
+        self.second[j][0].start()
+        add_into(self.grad.at[1, s, y, 1 - x], self.came1.at[1, s, 1 - x])
+        self.second[j][1].start()
+        add_into(self.grad.at[0, s, y, x], self.came1.at[0, s, y])
+        add_into(self.grad.at[1, s, y, x], self.came1.at[1, s, x])
+
+    def push3(self, j):
+        _, _, _, y, x = place()
+        s = self.slot(j)
+        self.second_all[j].wait_recv()
+        for half in (0, 1):
+            add_into(self.grad.at[half, s, y, x], self.came2.at[half, s])
+        self.send_on(j)
+
+    def send_on(self, j):
+        if j > 0:
+            self.third[j - 1].start()
+
+    def all1(self):
+        for j in self.order:
+            self.push1(j)
+
+    def all2(self):
+        for j in self.order:
+            self.push2(j)
+
+    def all3(self):
+        for j in self.order:
+            self.push3(j)
+
+    def done(self):
+        self.third_all.wait_recv()
+
+    def sent(self):
+        for copy in self.third:
+            copy.wait_send()
+        self.sent_rest()
+
+    def sent_rest(self):
+        self.first_sent.wait_send()
+        self.second_sent.wait_send()
+
+    def result(self, half):
+        _, _, _, y, x = place()
+        total = self.grad[half, self.slot(0), y, x].astype(F32)
+        for k in range(3):
+            total = total + self.came3[k, half].astype(F32)
+        return total
+
+
+class HalfScatter(Scatter):
+    order = (1, 0)
+
+    def slot(self, j):
+        return half_slot(j)
+
+    def third_slot(self, j):
+        return j % 2
+
+    def send_on(self, j):
+        if j == 1:
+
+            @pl.when(is_active())
+            def _():
+                self.third[0].start()
+
+        @pl.when(is_passive())
+        def _():
+            self.third[1 + j].start()
+
+    def done(self):
+        @pl.when(is_active())
+        def _():
+            self.third_all.wait_recv()
+
+    def sent(self):
+        @pl.when(is_active())
+        def _():
+            self.third[0].wait_send()
+
+        @pl.when(is_passive())
+        def _():
+            self.third[1].wait_send()
+            self.third[2].wait_send()
+
+        self.sent_rest()
+
+
+class SmallScatter:
+    def __init__(self, sems, grad, came_z, came_y, came_x):
+        c, _, z, y, x = place()
+        self.grad, self.came_z, self.came_y, self.came_x = grad, came_z, came_y, came_x
+        got = sems.new_receive()
+        self.first = [
+            sems.copy(
+                grad.at[half_slot(j % 2)],
+                came_z.at[j - 1],
+                c,
+                chip(partner(z, j), y, x),
+                None,
+                got,
+            )
+            for j in (1, 2, 3)
+        ]
+        self.first_all = joint(came_z, (sems.new_send(), got))
+        s = half_slot(0)
+        self.second = sems.copy(grad.at[s, 1 - y], came_y, c, chip(z, 1 - y, x))
+        self.third = sems.copy(grad.at[s, y, 1 - x], came_x, c, chip(z, y, 1 - x))
+
+    def push1(self):
+        @pl.when(is_active())
+        def _():
+            self.first[0].start()
+
+        @pl.when(is_passive())
+        def _():
+            self.first[1].start()
+            self.first[2].start()
+
+    def push2(self):
+        _, _, _, y, _ = place()
+        s = half_slot(0)
+
+        @pl.when(is_active())
+        def _():
+            self.first_all.wait_recv()
+            for row in (1 - y, y):
+                total = self.grad[s, row].astype(F32)
+                for k in range(3):
+                    total = total + self.came_z[k, row].astype(F32)
+                self.grad[s, row] = total.astype(BF16)
+            self.second.start()
+
+    def push3(self):
+        _, _, _, y, _ = place()
+        s = half_slot(0)
+
+        @pl.when(is_active())
+        def _():
+            self.second.wait_recv()
+            add_into(self.grad.at[s, y], self.came_y)
+            self.third.start()
+
+    def result(self):
+        _, _, _, y, x = place()
+        self.third.wait_recv()
+        return self.grad[half_slot(0), y, x].astype(F32) + self.came_x[...].astype(F32)
+
+    def sent(self):
+        @pl.when(is_active())
+        def _():
+            for copy in (self.first[0], self.second, self.third):
+                copy.wait_send()
+
+        @pl.when(is_passive())
+        def _():
+            self.first[1].wait_send()
+            self.first[2].wait_send()
+
+
+class Transpose:
+    def __init__(self, sems, source, target):
+        c, seq, _, _, _ = place()
+        self.source, self.target = source, target
+        pair = (sems.new_send(), sems.new_receive())
+        self.copies = [
+            sems.copy(source.at[(seq + k) % 16], target.at[seq], c, (seq + k) % 16, *pair)
+            for k in range(1, 16)
+        ]
+        self.all = joint(target.at[pl.ds(0, 15)], pair)
+
+    def start(self):
+        _, seq, _, _, _ = place()
+        for copy in self.copies:
+            copy.start()
+        self.target[seq] = self.source[seq]
+
+    def done(self):
+        self.all.wait()
+
+
+def wide(tile, count=WIDE // LANES):
+    return jnp.concatenate([tile] * count, axis=1)
+
+
+def rows_of(ref, base):
+    return jnp.broadcast_to(ref[pl.ds(base, 1), :], (16, LANES))
+
+
+def spread(slab, j):
+    return jnp.broadcast_to(slab[j : j + 1, :], (16, slab.shape[1]))
+
+
+def put_partial(ref, j, value):
+    folded = value[:8] + value[8:]
+    for g in range(WIDE // LANES):
+        ref[pl.ds(g * 64 + 8 * j, 8), :] = folded[:, g * LANES : (g + 1) * LANES]
+
+
+def take_partial(ref):
+    out = []
+    for g in range(WIDE // LANES):
+        total = ref[pl.ds(g * 64, 8, stride=8), :]
+        for j in range(1, 8):
+            total = total + ref[pl.ds(g * 64 + j, 8, stride=8), :]
+        out.append(total)
+    return jnp.concatenate(out, axis=1)
+
+
+def fold_lanes(value):
+    total = value[:, :LANES]
+    for g in range(1, value.shape[1] // LANES):
+        total = total + value[:, g * LANES : (g + 1) * LANES]
+    return total
+
+
+def dot_nn(a, b):
+    return jnp.dot(a, b, preferred_element_type=F32)
+
+
+def dot_nt(a, b):
+    return lax.dot_general(a, b, contract_last, preferred_element_type=F32)
+
+
+def dot_tn(a, b):
+    return lax.dot_general(a, b, contract_first, preferred_element_type=F32)
+
+
+def for_each(count, body):
+    def step(i, carry):
+        body(i)
+        return carry
+
+    lax.fori_loop(0, count, step, 0)
+
+
+def lanes_at(i, width):
+    return pl.ds(pl.multiple_of(i * width, width), width)
+
+
+def fused_kernel(
+    valid,
+    hid,
+    out_g,
+    resets,
+    in_w,
+    out_w,
+    x_w,
+    dt_w,
+    a_log,
+    conv_w,
+    vectors,
+    o_out,
+    o_gh,
+    o_gin,
+    o_gout,
+    o_small,
+    o_gain,
+    hidb,
+    gbr,
+    kb,
+    gain_b,
+    nrm,
+    nrm_t,
+    xext,
+    sig,
+    delta,
+    zz,
+    gs,
+    yy,
+    bb,
+    cb,
+    a2,
+    prm,
+    hs,
+    qb,
+    qc,
+    part1,
+    part2,
+    part3,
+    gbc,
+    low,
+    mid,
+    mid_t,
+    gz,
+    wx,
+    wz,
+    wo,
+    wp,
+    gx_w,
+    gz_w,
+    go_w,
+    gp_w,
+    x1,
+    x2,
+    x3,
+    z1,
+    z2,
+    z3,
+    o1,
+    o2,
+    o3,
+    p1,
+    p2,
+    p3,
+    hp,
+    hpr,
+    hret,
+    hin,
+    lp,
+    lpr,
+    xd_out,
+    xd_in,
+    gext,
+    gedge,
+    rowx,
+    rowx_in,
+    fin,
+    fin_in,
+    fsm,
+    send_sems,
+    recv_sems,
+):
+    c, seq, z, y, x = place()
+    mate = 1 - c
+    after = (seq + 1) % 16
+    before = (seq + 15) % 16
+    sems = Semaphores(send_sems, recv_sems)
+
+    barrier = pltpu.get_barrier_semaphore()
+    for k in range(1, 16):
+        pl.semaphore_signal(
+            barrier, inc=1, device_id=(c, (seq + k) % 16), device_id_type=MESH
+        )
+    pl.semaphore_signal(barrier, inc=1, device_id=(mate, seq), device_id_type=MESH)
+    pl.semaphore_signal(barrier, inc=1, device_id=(mate, after), device_id_type=MESH)
+    pl.semaphore_signal(barrier, inc=1, device_id=(mate, before), device_id_type=MESH)
+
+    for half in (0, 1):
+        wx[half, z, y, x] = in_w[:, pl.ds(pl.multiple_of(c * 1024 + half * 512, 512), 512)]
+        wz[half, z, y, x] = in_w[
+            :, pl.ds(pl.multiple_of(2048 + c * 1024 + half * 512, 512), 512)
+        ]
+
+    @pl.when(z // 2 == c)
+    def _():
+        for half in (0, 1):
+            wo[half, z % 2, y, x] = out_w[:, half * 512 : (half + 1) * 512]
+        wp[z % 2, y, x, 0:96, :] = x_w[...]
+        wp[z % 2, y, x, 96:160, :] = dt_w[...]
+        wp[z % 2, y, x, 160:176, :] = a_log[...]
+        wp[z % 2, y, x, 176:192, :] = jnp.concatenate(
+            [conv_w[...].astype(F32), vectors[0:3, :], jnp.zeros((9, LANES), F32)], axis=0
+        ).astype(BF16)
+
+    lane = lax.broadcasted_iota(jnp.int32, (8, LANES), 1)
+    gain_mine = jnp.where(lane // 64 == x, jnp.broadcast_to(vectors[3:4, :], (8, LANES)), 0.0)
+    gain_b[seq] = gain_mine
+    kb[c] = jnp.transpose(
+        jnp.broadcast_to(1.0 - resets[...].astype(F32), (ROWS, LANES))
+    )
+    row_place = seq * ROWS + lax.broadcasted_iota(jnp.int32, (ROWS, LANES), 0)
+    live = (row_place < valid[0]).astype(F32)
+    hidb[c, pl.ds(16, ROWS), :] = hid[...]
+    for g in range(GROUPS):
+        at = slice(g * LANES, (g + 1) * LANES)
+        gbr[c, :, at] = (live * out_g[:, at].astype(F32)).astype(BF16)
+
+    pl.semaphore_wait(barrier, 18)
+
+    gather_x = Gather(sems, wx)
+    gather_z = Gather(sems, wz)
+    gather_o = HalfGather(sems, wo)
+    gather_p = SmallGather(sems, wp)
+    gain_sems = (sems.new_send(), sems.new_receive())
+    gain_copies = [
+        sems.copy(gain_b.at[seq], gain_b.at[seq], c, (seq + k) % 16, *gain_sems)
+        for k in range(1, 16)
+    ]
+    gain_all = joint(gain_b.at[pl.ds(0, 15)], gain_sems)
+    hid_copies = [
+        sems.copy(hidb.at[c, pl.ds(16, ROWS), :], hidb.at[c, pl.ds(16, ROWS), :], mate, seq),
+        sems.copy(hidb.at[c, pl.ds(128, 16), :], hidb.at[c, pl.ds(0, 16), :], c, after),
+        sems.copy(hidb.at[c, pl.ds(128, 16), :], hidb.at[c, pl.ds(0, 16), :], mate, after),
+        sems.copy(kb.at[c], kb.at[c], mate, seq),
+    ]
+    gbr_copy = sems.copy(gbr.at[c], gbr.at[c], mate, seq)
+    for copy in hid_copies:
+        copy.start()
+    for copy in gain_copies:
+        copy.start()
+    gather_p.start()
+    gather_x.start()
+    gather_x.relay(0)
+
+    for copy in hid_copies:
+        copy.wait()
+    gather_p.relay()
+    gain_all.wait()
+    gain_row = jnp.concatenate(
+        [gain_b[2 * g][0:1, :] + gain_b[2 * g + 1][0:1, :] for g in range(GROUPS)], axis=1
+    )
+    for ctx in (0, 1):
+
+        def norm_rows(i):
+            at = pl.ds(pl.multiple_of(i * 16, 16), 16)
+            rows = hidb[ctx, at, :].astype(F32)
+            r = lax.rsqrt(jnp.mean(rows * rows, axis=1, keepdims=True) + epsilon)
+            nrm[ctx, at, :] = (rows * r * gain_row).astype(BF16)
+
+        for_each(9, norm_rows)
+    gather_p.cross()
+    gather_z.start()
+    for ctx in (0, 1):
+        for g in range(GROUPS):
+            at = slice(g * LANES, (g + 1) * LANES)
+            nrm_t[at, ctx * ROWS : (ctx + 1) * ROWS] = jnp.transpose(
+                nrm[ctx, 16:144, at].astype(F32)
+            ).astype(BF16)
+
+    gather_x.relay(1)
+    gather_x.cross(0)
+    gather_x.relay(2)
+    gather_x.cross(1)
+    gather_x.relay(3)
+    gather_o.start()
+    gather_x.cross(2)
+    gather_x.cross(3)
+    gbr_copy.start()
+    gather_z.relay(0)
+    gather_x.done()
+    gather_z.relay(1)
+    gather_z.cross(0)
+    first_chip = (seq > 0).astype(F32)
+    for half in (0, 1):
+
+        def x_columns(i):
+            rows = nrm[...].reshape(288, 1024)
+            w = wx[half, :, :, :, :, lanes_at(i, 256)].reshape(1024, 256)
+            got = dot_nn(rows, w).astype(BF16).astype(F32)
+            at = pl.ds(pl.multiple_of(half * 512 + i * 256, 256), 256)
+            for ctx in (0, 1):
+                xext[ctx, 0:16, at] = got[ctx * 144 : ctx * 144 + 16] * first_chip
+                xext[ctx, 16:144, at] = got[ctx * 144 + 16 : ctx * 144 + 144]
+
+        for_each(2, x_columns)
+
+    gather_z.relay(2)
+    gather_z.cross(1)
+    gather_p.done()
+    for j in range(GROUPS):
+        prm[:, j * LANES : (j + 1) * LANES] = wp[
+            j // 4, (j // 2) % 2, j % 2, 160:192, :
+        ].astype(F32)
+    a2[...] = -jnp.exp(prm[0:16, :]) * LOG2E
+
+    def conv_rows(ctx, at):
+        total = prm[20:21, at] + prm[16:17, at] * xext[ctx, 13:141, at]
+        for k in range(1, 4):
+            total = total + prm[16 + k : 17 + k, at] * xext[ctx, 13 + k : 141 + k, at]
+        return total
+
+    for ctx in (0, 1):
+
+        def conv_columns(i):
+            at = lanes_at(i, LANES)
+            total = conv_rows(ctx, at)
+            rows = slice(ctx * ROWS, (ctx + 1) * ROWS)
+            sig[rows, at] = (total * jax.nn.sigmoid(total)).astype(BF16)
+
+        for_each(GROUPS, conv_columns)
+
+    total = jnp.zeros((256, LANES), F32)
+    for j in range(GROUPS):
+        total = total + dot_nt(
+            sig[:, j * LANES : (j + 1) * LANES], wp[j // 4, (j // 2) % 2, j % 2, 0:128, :]
+        )
+    xd_out[...] = total
+    xd_copy = sems.copy(xd_out, xd_in, mate, seq)
+    xd_copy.start()
+    gather_z.relay(3)
+    gather_z.cross(2)
+    xd_copy.wait()
+    xd = xd_out[...] + xd_in[...]
+    low[...] = xd[:, 0:64].astype(BF16)
+    for n in range(16):
+        bb[pl.ds(n, 256, stride=16), :] = jnp.broadcast_to(xd[:, 64 + n : 65 + n], (256, LANES))
+        cb[pl.ds(n, 256, stride=16), :] = jnp.broadcast_to(xd[:, 80 + n : 81 + n], (256, LANES))
+    for j in range(GROUPS):
+        at = slice(j * LANES, (j + 1) * LANES)
+        pre = dot_nn(low[...], wp[j // 4, (j // 2) % 2, j % 2, 96:160, :]) + prm[21:22, at]
+        delta[:, at] = jnp.maximum(pre, 0.0) + jnp.log1p(jnp.exp(-jnp.abs(pre)))
+
+    gather_z.cross(3)
+    gather_o.relay(0)
+    gather_o.relay(1)
+
+    def decay(slab, j, a, base):
+        return jnp.exp2(spread(slab, j) * a) * wide(rows_of(kb2, base))
+
+    kb2 = kb.reshape(256, LANES)
+
+    def tile16(ref, t):
+        return ref[pl.ds(pl.multiple_of(t * 16, 16), 16), :]
+
+    def forward_ends(q):
+        ctx, block = q // 2, q % 2
+        at = lanes_at(block, WIDE)
+        a = a2[:, at]
+
+        def eight(i, h):
+            t0 = pl.multiple_of(ctx * ROWS + i * 8, 8)
+            d = delta[pl.ds(t0, 8), at]
+            u = d * slab_of(sig, t0, at)
+            for j in range(8):
+                h = decay(d, j, a, t0 + j) * h + spread(u, j) * wide(tile16(bb, t0 + j))
+            return h
+
+        h = lax.fori_loop(0, 16, eight, jnp.zeros((16, WIDE), F32))
+        rows = pl.ds(pl.multiple_of(ctx * ROWS, ROWS), ROWS)
+        summed = jnp.sum(delta[rows, at], axis=0, keepdims=True)
+        kept = jnp.min(kb[ctx], axis=0, keepdims=True)
+        decays = jnp.exp2(jnp.broadcast_to(summed, (16, WIDE)) * a) * wide(
+            jnp.broadcast_to(kept, (16, LANES))
+        )
+        for g in range(4):
+            piece = ctx * GROUPS + block * 4 + g
+            hp[piece, 0] = h[:, g * LANES : (g + 1) * LANES]
+            hp[piece, 1] = decays[:, g * LANES : (g + 1) * LANES]
+
+    def slab_of(ref, t0, at):
+        base = pl.multiple_of((t0 // 16) * 16, 16)
+        both = ref[pl.ds(base, 16), at].astype(F32)
+        return jnp.where(t0 % 16 == 0, both[:8], both[8:])
+
+    for_each(4, forward_ends)
+    send_ends = Transpose(sems, hp, hpr)
+    send_ends.start()
+    gather_z.done()
+
+    def z_columns(i):
+        rows = nrm_rows()
+        for half in (0, 1):
+            w = wz[half, :, :, :, :, lanes_at(i, 256)].reshape(1024, 256)
+            at = pl.ds(pl.multiple_of(half * 512 + i * 256, 256), 256)
+            zz[:, at] = dot_nn(rows, w)
+
+    def nrm_rows():
+        return jnp.concatenate([nrm[0, 16:144, :], nrm[1, 16:144, :]], axis=0)
+
+    for_each(2, z_columns)
+    gather_o.cross(0)
+    send_ends.done()
+    state = jnp.zeros((16, LANES), F32)
+    for s in range(16):
+        hret[s] = state
+        state = hpr[s, 1] * state + hpr[s, 0]
+    return_states = Transpose(sems, hret, hin)
+    return_states.start()
+    gather_o.cross(1)
+    return_states.done()
+
+    def forward(q):
+        ctx, block = q // 2, q % 2
+        at = lanes_at(block, WIDE)
+        a = a2[:, at]
+        h0 = jnp.concatenate([hin[ctx * GROUPS + block * 4 + g] for g in range(4)], axis=1)
+        hs[ctx * 129, :, at] = h0
+
+        def eight(i, h):
+            t0 = pl.multiple_of(ctx * ROWS + i * 8, 8)
+            d = delta[pl.ds(t0, 8), at]
+            s8 = slab_of(sig, t0, at)
+            u = d * s8
+            for j in range(8):
+                h = decay(d, j, a, t0 + j) * h + spread(u, j) * wide(tile16(bb, t0 + j))
+                hs[t0 + ctx + j + 1, :, at] = h
+                put_partial(part1, j, h * wide(tile16(cb, t0 + j)))
+            yy[pl.ds(t0, 8), at] = take_partial(part1) + prm[22:23, at] * s8
+            return h
+
+        lax.fori_loop(0, 16, eight, h0)
+
+    for_each(4, forward)
+
+    for ctx in (0, 1):
+        for g in range(GROUPS):
+            at = slice(g * LANES, (g + 1) * LANES)
+            rows = slice(ctx * ROWS, (ctx + 1) * ROWS)
+            zv = zz[rows, at]
+            val = (yy[rows, at] * zv * jax.nn.sigmoid(zv)).astype(BF16)
+            mid[rows, at] = val
+            mid_t[at, rows] = jnp.transpose(val.astype(F32)).astype(BF16)
+
+    gbr_copy.wait()
+
+    def out_grads(i):
+        e = pl.ds(pl.multiple_of(i * 256, 256), 256)
+        branch = gbr[...].reshape(256, 1024)
+        for half in (0, 1):
+            got = dot_nn(mid_t[e, :], branch[:, half * 512 : (half + 1) * 512])
+            go_w[half, i // 2, i % 2] = got.astype(BF16).reshape(2, 128, 512)
+
+    for_each(4, out_grads)
+    scatter_o = HalfScatter(sems, go_w, o1, o2, o3)
+    scatter_o.push1(1)
+
+    def branch_back(i):
+        branch = gbr[...].reshape(256, 1024)
+        w0 = wo[0, i // 2, i % 2].reshape(256, 512)
+        w1 = wo[1, i // 2, i % 2].reshape(256, 512)
+        gm = dot_nt(branch[:, :512], w0) + dot_nt(branch[:, 512:], w1)
+        at = lanes_at(i, 256)
+        zv = zz[:, at]
+        sigma = jax.nn.sigmoid(zv)
+        gs[:, at] = gm * (zv * sigma)
+        gz[:, at] = (gm * yy[:, at] * (sigma * (1.0 + zv * (1.0 - sigma)))).astype(BF16)
+
+
+    def z_grads(i):
+        d = pl.ds(pl.multiple_of(i * 128, 128), 128)
+        for half in (0, 1):
+            got = dot_nn(nrm_t[d, :], gz[:, half * 512 : (half + 1) * 512])
+            gz_w[half, i // 2, i % 2] = got.astype(BF16).reshape(2, 64, 512)
+
+    scatter_z = Scatter(sems, gz_w, z1, z2, z3)
+
+    def backward_ends(q):
+        ctx, block = q // 2, q % 2
+        at = lanes_at(block, WIDE)
+        a = a2[:, at]
+
+        def eight(i, adj):
+            t0 = pl.multiple_of(ctx * ROWS + (15 - i) * 8, 8)
+            d = delta[pl.ds(t0, 8), at]
+            u = gs[pl.ds(t0, 8), at]
+            for j in range(7, -1, -1):
+                adj = decay(d, j, a, t0 + j) * (adj + spread(u, j) * wide(tile16(cb, t0 + j)))
+            return adj
+
+        adj = lax.fori_loop(0, 16, eight, jnp.zeros((16, WIDE), F32))
+        for g in range(4):
+            lp[ctx * GROUPS + block * 4 + g] = adj[:, g * LANES : (g + 1) * LANES]
+
+    for j in (0, 1):
+        gather_o.slot_done(j)
+        block = half_slot(j)
+        branch_back(2 * block)
+        branch_back(2 * block + 1)
+        backward_ends(block)
+        backward_ends(2 + block)
+    send_adj = Transpose(sems, lp, lpr)
+    send_adj.start()
+    for_each(8, z_grads)
+    send_adj.done()
+    state = jnp.zeros((16, LANES), F32)
+    for s in range(15, -1, -1):
+        hret[s] = state
+        state = hpr[s, 1] * state + lpr[s]
+    return_adj = Transpose(sems, hret, hin)
+    return_adj.start()
+    scatter_o.push1(0)
+    scatter_z.push1(2)
+    scatter_z.push1(3)
+    for half in (0, 1):
+        got = dot_nn(mid[...], wo[half].reshape(1024, 512))
+        for ctx in (0, 1):
+            rowx[ctx, :, half * 512 : (half + 1) * 512] = got[ctx * ROWS : (ctx + 1) * ROWS]
+    rows_copy = sems.copy(rowx.at[mate], rowx_in.at[0], mate, seq)
+    rows_copy.start()
+    rows_copy.wait()
+    for g in range(GROUPS):
+        at = slice(g * LANES, (g + 1) * LANES)
+        o_out[:, at] = (
+            hid[:, at].astype(F32) + live * (rowx[c, :, at] + rowx_in[0, :, at])
+        ).astype(BF16)
+    return_adj.done()
+
+    sub = lax.broadcasted_iota(jnp.int32, (8, LANES), 0)
+    pick_b = [(lane == 64 + 8 * k + sub).astype(F32) for k in (0, 1)]
+    pick_c = [(lane == 80 + 8 * k + sub).astype(F32) for k in (0, 1)]
+    all_ones = jnp.ones((LANES, LANES), BF16)
+    def backward(ctx, block):
+        at = slice(block * WIDE, (block + 1) * WIDE)
+        a = a2[:, at]
+
+        def eight(i, carry):
+            adj, grad_a = carry
+            t0 = pl.multiple_of(ctx * ROWS + (15 - i) * 8, 8)
+            d = delta[pl.ds(t0, 8), at]
+            g8 = gs[pl.ds(t0, 8), at]
+            u = d * slab_of(sig, t0, at)
+            h_next = hs[t0 + ctx + 8, :, at]
+            for j in range(7, -1, -1):
+                t = t0 + j
+                dj = spread(d, j)
+                gj = spread(g8, j)
+                lam = adj + gj * wide(tile16(cb, t))
+                adj = jnp.exp2(dj * a) * wide(rows_of(kb2, t)) * lam
+                h_prev = hs[t + ctx, :, at]
+                flow = adj * h_prev
+                grad_a = grad_a + flow * dj
+                put_partial(part1, j, flow * a)
+                put_partial(part2, j, lam * wide(tile16(bb, t)))
+                to = pl.ds(pl.multiple_of((t - ctx * ROWS) * 16, 16), 16)
+                qb[block, to, :] = fold_lanes(lam * spread(u, j)).astype(BF16)
+                qc[block, to, :] = fold_lanes(gj * h_next).astype(BF16)
+                h_next = h_prev
+            yy[pl.ds(t0, 8), at] = take_partial(part1) * (1.0 / LOG2E)
+            zz[pl.ds(t0, 8), at] = take_partial(part2)
+            return adj, grad_a
+
+        adj0 = jnp.concatenate([hin[ctx * GROUPS + block * 4 + g] for g in range(4)], axis=1)
+        _, grad_a = lax.fori_loop(0, 16, eight, (adj0, jnp.zeros((16, WIDE), F32)))
+        hs[ctx * 129, :, at] = grad_a
+
+    def sum_lanes(ctx, i):
+        for k in range(2):
+            t0 = pl.multiple_of(i * 32 + k * 16, 16)
+            at = pl.ds(pl.multiple_of(t0 * 16, 256), 256)
+            sum_b = dot_nn(qb[0, at, :], all_ones) + dot_nn(qb[1, at, :], all_ones)
+            sum_c = dot_nn(qc[0, at, :], all_ones) + dot_nn(qc[1, at, :], all_ones)
+            for j in range(16):
+                got = sum_b[16 * j : 16 * j + 8] * pick_b[0]
+                got = got + sum_b[16 * j + 8 : 16 * j + 16] * pick_b[1]
+                got = got + sum_c[16 * j : 16 * j + 8] * pick_c[0]
+                got = got + sum_c[16 * j + 8 : 16 * j + 16] * pick_c[1]
+                part3[k * 128 + 8 * j : k * 128 + 8 * j + 8, :] = got
+            for j in range(2):
+                got = part3[pl.ds(k * 128 + j * 64, 8, stride=8), :]
+                for n in range(1, 8):
+                    got = got + part3[pl.ds(k * 128 + j * 64 + n, 8, stride=8), :]
+                gbc[pl.ds(pl.multiple_of(ctx * ROWS + t0 + 8 * j, 8), 8), :] = got
+
+    backward(0, 0)
+    scatter_o.push2(1)
+    scatter_z.push1(1)
+    scatter_z.push1(0)
+    backward(0, 1)
+    scatter_o.push2(0)
+    for_each(4, functools.partial(sum_lanes, 0))
+    backward(1, 0)
+    scatter_o.push3(1)
+    backward(1, 1)
+    scatter_z.push2(2)
+    for_each(4, functools.partial(sum_lanes, 1))
+
+    ones = []
+    for j in range(GROUPS):
+        at = slice(j * LANES, (j + 1) * LANES)
+        sv = sig[:, at].astype(F32)
+        g_pre = ((yy[:, at] + zz[:, at] * sv) * (1.0 - jnp.exp(-delta[:, at]))).astype(BF16)
+        mid[:, at] = g_pre
+        ones.append(jnp.sum(g_pre.astype(F32), axis=0, keepdims=True))
+    g_bdt = jnp.concatenate(ones, axis=1)
+
+    total = jnp.zeros((256, 64), F32)
+    for j in range(GROUPS):
+        total = total + dot_nt(
+            mid[:, j * LANES : (j + 1) * LANES], wp[j // 4, (j // 2) % 2, j % 2, 96:160, :]
+        )
+    xd_out[:, 0:64] = total
+    xd_out[:, 64:128] = gbc[:, 64:128]
+    gd_copy = sems.copy(xd_out, xd_in, mate, seq)
+    gd_copy.start()
+    scatter_z.push2(3)
+    gd_copy.wait()
+    g_dbl = (xd_out[...] + xd_in[...]).astype(BF16)
+
+    for ctx in (0, 1):
+        for j in range(GROUPS):
+            at = slice(j * LANES, (j + 1) * LANES)
+            rows = slice(ctx * ROWS, (ctx + 1) * ROWS)
+            back = dot_nn(g_dbl[rows, :], wp[j // 4, (j // 2) % 2, j % 2, 0:128, :])
+            g_sig = gs[rows, at] * prm[22:23, at] + zz[rows, at] * delta[rows, at] + back
+            v = conv_rows(ctx, at)
+            sigma = jax.nn.sigmoid(v)
+            gext[ctx, 0:128, at] = g_sig * (sigma * (1.0 + v * (1.0 - sigma)))
+    edge_copies = [
+        sems.copy(gext.at[ctx, pl.ds(0, 8), :], gedge.at[ctx], c, before) for ctx in (0, 1)
+    ]
+    for copy in edge_copies:
+        copy.start()
+    scatter_z.push2(1)
+    scatter_o.push3(0)
+
+    def small_grads():
+        a_rows = -jnp.exp(prm[0:16, :])
+        g_alog = (hs[0] + hs[129]) * a_rows
+        g_t = jnp.transpose(g_dbl.astype(F32))[0:96].astype(BF16)
+        low_t = jnp.transpose(
+            jnp.concatenate([low[...].astype(F32), jnp.zeros((256, 64), F32)], axis=1)
+        )[0:64].astype(BF16)
+        for j in range(GROUPS):
+            at = slice(j * LANES, (j + 1) * LANES)
+            to = (j // 4, (j // 2) % 2, j % 2)
+            sv = sig[:, at].astype(F32)
+            gp_w[to + (slice(0, 96),)] = dot_nn(g_t, sig[:, at]).astype(BF16)
+            g_dtw = dot_nn(low_t, mid[:, at])
+            taps = []
+            for k in range(4):
+                term = jnp.zeros((1, LANES), F32)
+                for ctx in (0, 1):
+                    term = term + jnp.sum(
+                        gext[ctx, 0:128, at] * xext[ctx, 13 + k : 141 + k, at],
+                        axis=0,
+                        keepdims=True,
+                    )
+                taps.append(term)
+            bias = jnp.sum(gext[0, 0:128, at] + gext[1, 0:128, at], axis=0, keepdims=True)
+            skip = jnp.sum(gs[:, at] * sv, axis=0, keepdims=True)
+            rest = jnp.concatenate(
+                [g_dtw, g_alog[:, at]]
+                + taps
+                + [bias, g_bdt[:, at], skip, jnp.zeros((9, LANES), F32)],
+                axis=0,
+            )
+            gp_w[to + (slice(96, 192),)] = rest.astype(BF16)
+
+    small_grads()
+    scatter_p = SmallScatter(sems, gp_w, p1, p2, p3)
+    scatter_p.push1()
+
+    for copy in edge_copies:
+        copy.wait()
+    last_chip = (seq < 15).astype(F32)
+    for ctx in (0, 1):
+        gext[ctx, 128:136, :] = gedge[ctx] * last_chip
+
+    for ctx in (0, 1):
+
+        def x_back(i):
+            at = lanes_at(i, LANES)
+            total = prm[19:20, at] * gext[ctx, 0:128, at]
+            for k in range(3):
+                total = total + prm[16 + k : 17 + k, at] * gext[ctx, 3 - k : 131 - k, at]
+            mid[ctx * ROWS : (ctx + 1) * ROWS, at] = total.astype(BF16)
+
+        for_each(GROUPS, x_back)
+
+    def x_grads(i):
+        d = pl.ds(pl.multiple_of(i * 128, 128), 128)
+        for half in (0, 1):
+            got = dot_nn(nrm_t[d, :], mid[:, half * 512 : (half + 1) * 512])
+            gx_w[half, i // 2, i % 2] = got.astype(BF16).reshape(2, 64, 512)
+
+    scatter_x = Scatter(sems, gx_w, x1, x2, x3)
+    scatter_z.push2(0)
+    for j in scatter_x.order:
+        zj = partner(z, j)
+        x_grads(2 * zj)
+        x_grads(2 * zj + 1)
+        scatter_x.push1(j)
+        scatter_z.push3(j)
+    def normed_back(i):
+        total = jnp.zeros((256, 128), F32)
+        for half in (0, 1):
+            at = slice(half * 512, (half + 1) * 512)
+            total = total + dot_nt(mid[:, at], wx[half, i // 2, i % 2].reshape(128, 512))
+            total = total + dot_nt(gz[:, at], wz[half, i // 2, i % 2].reshape(128, 512))
+        to = lanes_at(i, 128)
+        for ctx in (0, 1):
+            rowx[ctx, :, to] = total[ctx * ROWS : (ctx + 1) * ROWS]
+
+    for i in range(4):
+        normed_back(i)
+    scatter_x.push2(2)
+    for i in range(4, 8):
+        normed_back(i)
+    back_copy = sems.copy(rowx.at[mate], rowx_in.at[1], mate, seq)
+    back_copy.start()
+    scatter_x.push2(3)
+    scatter_x.push2(1)
+
+    def hidden_rows(i):
+        at = pl.ds(pl.multiple_of(i * 16, 16), 16)
+        rows = hid[at, :].astype(F32)
+        r = lax.rsqrt(jnp.mean(rows * rows, axis=1, keepdims=True) + epsilon)
+        g_hat = (rowx[c, at, :] + rowx_in[1, at, :]) * gain_row
+        inner = jnp.mean(g_hat * rows, axis=1, keepdims=True)
+        o_gh[at, :] = r * g_hat - rows * (r * r * r * inner) + out_g[at, :].astype(F32)
+
+    back_copy.wait()
+    for_each(8, hidden_rows)
+    scatter_x.push3(2)
+    scatter_x.push2(0)
+    scatter_x.push3(3)
+    scatter_x.push3(1)
+    scatter_p.push2()
+    scatter_x.push3(0)
+    scatter_o.done()
+    out_copy = sems.copy(o_gout, o_gout, mate, seq)
+
+    @pl.when(is_active())
+    def _():
+        for half in (0, 1):
+            o_gout[:, half * 512 : (half + 1) * 512] = scatter_o.result(half)
+        out_copy.start()
+
+    scatter_z.done()
+    for half in (0, 1):
+        fin[2 + half] = scatter_z.result(half)
+    z_copy = sems.copy(fin.at[pl.ds(2, 2)], fin_in.at[pl.ds(2, 2)], mate, seq)
+    z_copy.start()
+    scatter_p.push3()
+    small_copy = sems.copy(fsm, fsm, mate, seq)
+
+    @pl.when(is_active())
+    def _():
+        fsm[...] = scatter_p.result()
+        small_copy.start()
+
+    def weight_rows(part, gain_sum):
+        for half in (0, 1):
+            for core, ref in ((c, fin), (mate, fin_in)):
+                at = pl.ds(pl.multiple_of(part * 2048 + core * 1024 + half * 512, 512), 512)
+                rows = ref[part * 2 + half]
+                o_gin[:, at] = rows
+                gain_sum = gain_sum + fold_lanes(rows * in_w[:, at].astype(F32))
+        return gain_sum
+
+    z_copy.wait()
+    gain_sum = weight_rows(1, jnp.zeros((64, LANES), F32))
+    for group in (gather_x, gather_z, gather_o, gather_p, scatter_z, scatter_o):
+        group.sent()
+
+    scatter_x.done()
+    for half in (0, 1):
+        fin[half] = scatter_x.result(half)
+    x_copy = sems.copy(fin.at[pl.ds(0, 2)], fin_in.at[pl.ds(0, 2)], mate, seq)
+    x_copy.start()
+
+    @pl.when(is_active())
+    def _():
+        out_copy.wait_send()
+        small_copy.wait_send()
+
+    @pl.when(is_passive())
+    def _():
+        out_copy.wait_recv()
+        small_copy.wait_recv()
+
+    o_small[...] = fsm[...]
+    scatter_x.sent()
+    scatter_p.sent()
+    x_copy.wait()
+    o_gain[...] = weight_rows(0, gain_sum)
+
+
+def fused_shards(
+    hidden,
+    out_grad,
+    resets,
+    valid,
+    norm_gain,
+    in_weight,
+    conv_weight,
+    conv_bias,
+    x_weight,
+    dt_weight,
+    dt_bias,
+    a_log,
+    skip_gain,
+    out_weight,
+):
+    norm_row = norm_gain.astype(F32)
+    vectors = jnp.stack(
+        [
+            conv_bias.astype(F32),
+            dt_bias.astype(F32),
+            skip_gain.astype(F32),
+            jnp.concatenate([norm_row, norm_row]),
+        ]
+    )
+    vmem = pltpu.VMEM
+    count = 88
+    scratch = [
+        vmem((2, 144, 1024), BF16),
+        vmem((2, 128, 1024), BF16),
+        vmem((2, 128, LANES), F32),
+        vmem((16, 8, LANES), F32),
+        vmem((2, 144, 1024), BF16),
+        vmem((1024, 256), BF16),
+        vmem((2, 144, 1024), F32),
+        vmem((256, 1024), BF16),
+        vmem((256, 1024), F32),
+        vmem((256, 1024), F32),
+        vmem((256, 1024), F32),
+        vmem((256, 1024), F32),
+        vmem((4096, LANES), F32),
+        vmem((4096, LANES), F32),
+        vmem((16, 1024), F32),
+        vmem((32, 1024), F32),
+        vmem((258, 16, 1024), F32),
+        vmem((2, 2048, LANES), BF16),
+        vmem((2, 2048, LANES), BF16),
+        vmem((256, LANES), F32),
+        vmem((256, LANES), F32),
+        vmem((256, LANES), F32),
+        vmem((256, LANES), F32),
+        vmem((256, 64), BF16),
+        vmem((256, 1024), BF16),
+        vmem((1024, 256), BF16),
+        vmem((256, 1024), BF16),
+        vmem((2, 4, 2, 2, 64, 512), BF16),
+        vmem((2, 4, 2, 2, 64, 512), BF16),
+        vmem((2, 2, 2, 2, 128, 512), BF16),
+        vmem((2, 2, 2, 192, LANES), BF16),
+        vmem((2, 4, 2, 2, 64, 512), BF16),
+        vmem((2, 4, 2, 2, 64, 512), BF16),
+        vmem((2, 2, 2, 2, 128, 512), BF16),
+        vmem((2, 2, 2, 192, LANES), BF16),
+    ]
+    for z_count, rows, columns in ((4, 64, 512), (4, 64, 512), (2, 128, 512)):
+        scratch += [
+            vmem((2, z_count, 2, rows, columns), BF16),
+            vmem((2, z_count, rows, columns), BF16),
+            vmem((3, 2, rows, columns), BF16),
+        ]
+    scratch += [
+        vmem((3, 2, 2, 192, LANES), BF16),
+        vmem((2, 192, LANES), BF16),
+        vmem((192, LANES), BF16),
+        vmem((16, 2, 16, LANES), F32),
+        vmem((16, 2, 16, LANES), F32),
+        vmem((16, 16, LANES), F32),
+        vmem((16, 16, LANES), F32),
+        vmem((16, 16, LANES), F32),
+        vmem((16, 16, LANES), F32),
+        vmem((256, LANES), F32),
+        vmem((256, LANES), F32),
+        vmem((2, 136, 1024), F32),
+        vmem((2, 8, 1024), F32),
+        vmem((2, 128, 1024), F32),
+        vmem((2, 128, 1024), F32),
+        vmem((4, 64, 512), F32),
+        vmem((4, 64, 512), F32),
+        vmem((192, LANES), F32),
+        pltpu.SemaphoreType.DMA((count,)),
+        pltpu.SemaphoreType.DMA((count,)),
+    ]
+    whole = pl.BlockSpec(memory_space=pltpu.VMEM)
+    parts = pl.pallas_call(
+        fused_kernel,
+        out_shape=(
+            jax.ShapeDtypeStruct((128, 1024), BF16),
+            jax.ShapeDtypeStruct((128, 1024), F32),
+            jax.ShapeDtypeStruct((64, 4096), F32),
+            jax.ShapeDtypeStruct((128, 1024), F32),
+            jax.ShapeDtypeStruct((192, LANES), F32),
+            jax.ShapeDtypeStruct((64, LANES), F32),
+        ),
+        in_specs=[pl.BlockSpec(memory_space=pltpu.SMEM)] + [whole] * 10,
+        out_specs=(whole,) * 6,
+        scratch_shapes=scratch,
+        compiler_params=pltpu.CompilerParams(
+            collective_id=0, has_side_effects=True, vmem_limit_bytes=64 * 2**20
+        ),
+    )(
+        valid,
+        hidden[0],
+        out_grad[0],
+        resets,
+        in_weight,
+        out_weight,
+        x_weight.T,
+        dt_weight.T,
+        a_log.T,
+        conv_weight.T,
+        vectors,
+    )
+    got = pl.pallas_call(
+        place_outputs,
+        out_shape=tuple(
+            jax.ShapeDtypeStruct(shape, dtype)
+            for shape, dtype in (
+                ((128, 1024), BF16),
+                ((128, 1024), F32),
+                ((1, 64), F32),
+                ((64, 4096), F32),
+                ((4, LANES), F32),
+                ((1, LANES), F32),
+                ((96, LANES), F32),
+                ((64, LANES), F32),
+                ((1, LANES), F32),
+                ((16, LANES), F32),
+                ((1, LANES), F32),
+                ((128, 1024), F32),
+            )
+        ),
+        in_specs=[whole] * 7,
+        out_specs=(whole,) * 12,
+        compiler_params=pltpu.CompilerParams(vmem_limit_bytes=64 * 2**20),
+    )(*parts, vectors)
+    return (
+        got[0][None],
+        got[1][None],
+        got[2][0],
+        got[3],
+        got[4].T,
+        got[5][0],
+        got[6].T,
+        got[7].T,
+        got[8][0],
+        got[9].T,
+        got[10][0],
+        got[11],
+    )
+
+
+def place_outputs(
+    out,
+    g_hidden,
+    g_in,
+    g_out,
+    small,
+    gain,
+    vectors,
+    o_out,
+    o_hidden,
+    o_gain,
+    o_in,
+    o_taps,
+    o_bias,
+    o_xw,
+    o_dtw,
+    o_dtb,
+    o_alog,
+    o_skip,
+    o_outw,
+):
+    o_out[...] = out[...]
+    o_hidden[...] = g_hidden[...]
+    o_in[...] = g_in[...]
+    o_outw[...] = g_out[...]
+    o_xw[...] = small[0:96, :]
+    o_dtw[...] = small[96:160, :]
+    o_alog[...] = small[160:176, :]
+    o_taps[...] = small[176:180, :]
+    o_bias[...] = small[180:181, :]
+    o_dtb[...] = small[181:182, :]
+    o_skip[...] = small[182:183, :]
+    turned = jnp.transpose(jnp.concatenate([gain[...], jnp.zeros((64, LANES), F32)], axis=0))
+    o_gain[...] = (jnp.sum(turned, axis=0, keepdims=True) / vectors[3:4, :])[:, 0:64]
+
+
 def solution(mesh):
+    sizes = dict(mesh.shape)
+    body = fused_shards if sizes == {"ctx": 2, "seq": 16} else shards
     return jax.shard_map(
-        shards,
+        body,
         mesh=mesh,
         in_specs=(
             P("ctx", "seq", None),

time: 1970 us -> 166 us (0.08)
  waiting for transfers between devices: 828 us -> 0 us
  blocking collectives: 414 us -> 0 us
  other arithmetic: 390 us -> 0.66 us
  local copies, waits for them, and re-layouts: 181 us -> 1.26 us
  Pallas kernels: 0 us -> 162 us
  matrix products: 97.4 us -> 0 us
  loops' own time: 20 us -> 0 us
    reduce_scatter x5 -> x0, waiting for transfers between devices: 774 us -> none  [the longest x4 423 us: shards(): lax.psum_scatter((g_wconv, g_bconv, xw_rows, dtw_rows, g_bdt, g_alog, g_s...]
    all_gather x7 -> x0, blocking collectives: 265 us -> none  [the longest x1 41.5 us: shards(): lax.all_gather(dt_weight, 'seq', axis=0, tiled=True)]
    while x186 -> x0, other arithmetic: 196 us -> none
    pallas_call x0 -> x2, Pallas kernels: none -> 162 us  [the longest x1 159 us: fused_shards(): pl.pallas_call(fused_kernel, out_shape=(jax.ShapeDtypeStruct((128, 1024),...]
    unnamed x2 -> x0, blocking collectives: 149 us -> none
    dot_general x18 -> x0, matrix products: 97.4 us -> none  [the longest x2 23.5 us: backward_step(): g_binput = jnp.einsum('qen,qe->qn', adjoints, drive_blk, precision=highest)]
    reduce_sum x56 -> x0, other arithmetic: 92.4 us -> none  [the longest x48 47.6 us: token_step(): return (state_next, jnp.sum(state_next * coutput_now[None, :], -1))]
    psum x2 -> x0, waiting for transfers between devices: 47.6 us -> none  [shards(): lax.psum((g_gain_rows, g_win_rows, g_wconv_rows, g_bconv_rows, g_wx_rows,...]
  transfers between devices with their start and end apart: 15 -> 0, of which waited for: 8 -> 0; matrix products, arithmetic and copies ran while one was open for 10% -> 0% of each run, Pallas kernels for 0% -> 0%
where the time goes in v1:
time: 166 us
  Pallas kernels  162 us (98%)
    pallas_call x1, Pallas kernels, fused_shards(): pl.pallas_call(fused_kernel, out_shape=(jax.ShapeDtypeStruct((128, 1024),...  159 us

profile of v1, /device:TPU:0, one launch (start us, length us, event | category | flops | bytes accessed | tf_op | source)
XLA Modules:
  0.0 165.7 jit_solution(10493411481718877179)
XLA Ops:
  1.3 0.0 copy-start.3
  1.3 0.6 copy-done.3
  1.9 0.0 copy-start
  1.9 0.0 copy-start.1
  2.0 0.0 copy-start.2
  2.0 0.1 maximum_bitcast_fusion
  2.0 0.6 copy-done
  2.6 0.0 copy-done.1
  2.6 0.0 copy-done.2
  2.6 0.6 maximum_convert_fusion.vectors
  3.2 159.3 %shard_map.229 = (bf16[128,1024]{1,0:T(8,128)(2,1)}, f32[128,1024]{1,0:T(8,128)}, f32[64,4096]{1,0:T(8,128)}, f32[128,1024]{1,0:T(8,128)}, f32[192,128]{1,0:T(8,128)}, /*index=5*/f32[64,128]{1,0:T(8,128)}) custom-call(s32[1]{0:T(128)S(6)} %copy.26.valid, bf16[128,1024]{1,0:T(8,128)(2,1)} %bitcast.21, bf16[128,1024]{1,0:T(8,128)(2,1)} %bitcast.22, ...), custom_call_target="tpu_custom_call" | custom-call | tf_op jit(solution)/shard_map/pallas_call | solution.py:1697
  162.5 3.2 %shard_map.230 = (bf16[128,1024]{1,0:T(8,128)(2,1)}, f32[128,1024]{1,0:T(8,128)}, f32[1,64]{1,0:T(1,128)}, f32[64,4096]{1,0:T(8,128)}, f32[4,128]{1,0:T(4,128)},...) custom-call(bf16[128,1024]{1,0:T(8,128)(2,1)} %get-tuple-element.30., ...), custom_call_target="tpu_custom_call" | custom-call | tf_op jit(solution)/shard_map/pallas_call | solution.py:1726
Async XLA Ops:
  1.3 0.7 copy-start.3
  1.9 0.7 copy-start
  1.9 0.7 copy-start.1
  2.0 0.7 copy-start.2

commit v2 on v1

--- a/solution.py
+++ b/solution.py
@@ -544,51 +544,6 @@
                 copy.wait_send()
 
         self.sent_rest()
-
-
-class SmallGather:
-    def __init__(self, sems, buf):
-        c, _, z, y, x = place()
-        s = half_slot(0)
-        self.first = sems.copy(buf.at[s, y, x], buf.at[s, y, x], c, chip(z, y, 1 - x))
-        self.second = sems.copy(buf.at[s, y], buf.at[s, y], c, chip(z, 1 - y, x))
-        self.third = [
-            sems.copy(buf.at[s], buf.at[s], c, chip(partner(z, j), y, x)) for j in (1, 2, 3)
-        ]
-
-    def start(self):
-        @pl.when(is_active())
-        def _():
-            self.first.start()
-
-    def relay(self):
-        @pl.when(is_active())
-        def _():
-            self.first.wait_recv()
-            self.second.start()
-
-    def cross(self):
-        @pl.when(is_active())
-        def _():
-            self.second.wait_recv()
-            for copy in self.third:
-                copy.start()
-
-    def done(self):
-        @pl.when(is_active())
-        def _():
-            self.third[0].wait_recv()
-
-        @pl.when(is_passive())
-        def _():
-            self.third[1].wait_recv()
-            self.third[2].wait_recv()
-
-    def sent(self):
-        @pl.when(is_active())
-        def _():
-            for copy in [self.first, self.second] + self.third:
-                copy.wait_send()
 
 
 def add_into(total, part):
@@ -740,78 +695,6 @@
         self.sent_rest()
 
 
-class SmallScatter:
-    def __init__(self, sems, grad, came_z, came_y, came_x):
-        c, _, z, y, x = place()
-        self.grad, self.came_z, self.came_y, self.came_x = grad, came_z, came_y, came_x
-        got = sems.new_receive()
-        self.first = [
-            sems.copy(
-                grad.at[half_slot(j % 2)],
-                came_z.at[j - 1],
-                c,
-                chip(partner(z, j), y, x),
-                None,
-                got,
-            )
-            for j in (1, 2, 3)
-        ]
-        self.first_all = joint(came_z, (sems.new_send(), got))
-        s = half_slot(0)
-        self.second = sems.copy(grad.at[s, 1 - y], came_y, c, chip(z, 1 - y, x))
-        self.third = sems.copy(grad.at[s, y, 1 - x], came_x, c, chip(z, y, 1 - x))
-
-    def push1(self):
-        @pl.when(is_active())
-        def _():
-            self.first[0].start()
-
-        @pl.when(is_passive())
-        def _():
-            self.first[1].start()
-            self.first[2].start()
-
-    def push2(self):
-        _, _, _, y, _ = place()
-        s = half_slot(0)
-
-        @pl.when(is_active())
-        def _():
-            self.first_all.wait_recv()
-            for row in (1 - y, y):
-                total = self.grad[s, row].astype(F32)
-                for k in range(3):
-                    total = total + self.came_z[k, row].astype(F32)
-                self.grad[s, row] = total.astype(BF16)
-            self.second.start()
-
-    def push3(self):
-        _, _, _, y, _ = place()
-        s = half_slot(0)
-
-        @pl.when(is_active())
-        def _():
-            self.second.wait_recv()
-            add_into(self.grad.at[s, y], self.came_y)
-            self.third.start()
-
-    def result(self):
-        _, _, _, y, x = place()
-        self.third.wait_recv()
-        return self.grad[half_slot(0), y, x].astype(F32) + self.came_x[...].astype(F32)
-
-    def sent(self):
-        @pl.when(is_active())
-        def _():
-            for copy in (self.first[0], self.second, self.third):
-                copy.wait_send()
-
-        @pl.when(is_passive())
-        def _():
-            self.first[1].wait_send()
-            self.first[2].wait_send()
-
-
 class Transpose:
     def __init__(self, sems, source, target):
         c, seq, _, _, _ = place()
@@ -830,7 +713,10 @@
         self.target[seq] = self.source[seq]
 
     def done(self):
-        self.all.wait()
+        self.all.wait_recv()
+
+    def sent(self):
+        self.all.wait_send()
 
 
 def wide(tile, count=WIDE // LANES):
@@ -961,6 +847,8 @@
     hpr,
     hret,
     hin,
+    lret,
+    lin,
     lp,
     lpr,
     xd_out,
@@ -1000,10 +888,10 @@
     def _():
         for half in (0, 1):
             wo[half, z % 2, y, x] = out_w[:, half * 512 : (half + 1) * 512]
-        wp[z % 2, y, x, 0:96, :] = x_w[...]
-        wp[z % 2, y, x, 96:160, :] = dt_w[...]
-        wp[z % 2, y, x, 160:176, :] = a_log[...]
-        wp[z % 2, y, x, 176:192, :] = jnp.concatenate(
+        wp[0, z % 2, y, x] = x_w[...]
+        wp[1, z % 2, y, x, 0:64, :] = dt_w[...]
+        wp[1, z % 2, y, x, 64:80, :] = a_log[...]
+        wp[1, z % 2, y, x, 80:96, :] = jnp.concatenate(
             [conv_w[...].astype(F32), vectors[0:3, :], jnp.zeros((9, LANES), F32)], axis=0
         ).astype(BF16)
 
@@ -1025,7 +913,7 @@
     gather_x = Gather(sems, wx)
     gather_z = Gather(sems, wz)
     gather_o = HalfGather(sems, wo)
-    gather_p = SmallGather(sems, wp)
+    gather_p = HalfGather(sems, wp)
     gain_sems = (sems.new_send(), sems.new_receive())
     gain_copies = [
         sems.copy(gain_b.at[seq], gain_b.at[seq], c, (seq + k) % 16, *gain_sems)
@@ -1048,9 +936,10 @@
     gather_x.relay(0)
 
     for copy in hid_copies:
-        copy.wait()
-    gather_p.relay()
-    gain_all.wait()
+        copy.wait_recv()
+    gather_p.relay(0)
+    gather_p.relay(1)
+    gain_all.wait_recv()
     gain_row = jnp.concatenate(
         [gain_b[2 * g][0:1, :] + gain_b[2 * g + 1][0:1, :] for g in range(GROUPS)], axis=1
     )
@@ -1063,7 +952,8 @@
             nrm[ctx, at, :] = (rows * r * gain_row).astype(BF16)
 
         for_each(9, norm_rows)
-    gather_p.cross()
+    gather_p.cross(0)
+    gather_p.cross(1)
     gather_z.start()
     for ctx in (0, 1):
         for g in range(GROUPS):
@@ -1104,7 +994,7 @@
     gather_p.done()
     for j in range(GROUPS):
         prm[:, j * LANES : (j + 1) * LANES] = wp[
-            j // 4, (j // 2) % 2, j % 2, 160:192, :
+            1, j // 4, (j // 2) % 2, j % 2, 64:96, :
         ].astype(F32)
     a2[...] = -jnp.exp(prm[0:16, :]) * LOG2E
 
@@ -1124,12 +1014,13 @@
 
         for_each(GROUPS, conv_columns)
 
-    total = jnp.zeros((256, LANES), F32)
+    total = jnp.zeros((256, 96), F32)
     for j in range(GROUPS):
         total = total + dot_nt(
-            sig[:, j * LANES : (j + 1) * LANES], wp[j // 4, (j // 2) % 2, j % 2, 0:128, :]
+            sig[:, j * LANES : (j + 1) * LANES], wp[0, j // 4, (j // 2) % 2, j % 2]
         )
-    xd_out[...] = total
+    xd_out[:, 0:96] = total
+    xd_out[:, 96:128] = jnp.zeros((256, 32), F32)
     xd_copy = sems.copy(xd_out, xd_in, mate, seq)
     xd_copy.start()
     gather_z.relay(3)
@@ -1142,12 +1033,10 @@
         cb[pl.ds(n, 256, stride=16), :] = jnp.broadcast_to(xd[:, 80 + n : 81 + n], (256, LANES))
     for j in range(GROUPS):
         at = slice(j * LANES, (j + 1) * LANES)
-        pre = dot_nn(low[...], wp[j // 4, (j // 2) % 2, j % 2, 96:160, :]) + prm[21:22, at]
+        pre = dot_nn(low[...], wp[1, j // 4, (j // 2) % 2, j % 2, 0:64, :]) + prm[21:22, at]
         delta[:, at] = jnp.maximum(pre, 0.0) + jnp.log1p(jnp.exp(-jnp.abs(pre)))
 
     gather_z.cross(3)
-    gather_o.relay(0)
-    gather_o.relay(1)
 
     def decay(slab, j, a, base):
         return jnp.exp2(spread(slab, j) * a) * wide(rows_of(kb2, base))
@@ -1190,6 +1079,8 @@
     for_each(4, forward_ends)
     send_ends = Transpose(sems, hp, hpr)
     send_ends.start()
+    gather_o.relay(0)
+    gather_o.relay(1)
     gather_z.done()
 
     def z_columns(i):
@@ -1203,7 +1094,6 @@
         return jnp.concatenate([nrm[0, 16:144, :], nrm[1, 16:144, :]], axis=0)
 
     for_each(2, z_columns)
-    gather_o.cross(0)
     send_ends.done()
     state = jnp.zeros((16, LANES), F32)
     for s in range(16):
@@ -1211,8 +1101,8 @@
         state = hpr[s, 1] * state + hpr[s, 0]
     return_states = Transpose(sems, hret, hin)
     return_states.start()
+    gather_o.cross(0)
     gather_o.cross(1)
-    return_states.done()
 
     def forward(q):
         ctx, block = q // 2, q % 2
@@ -1235,29 +1125,7 @@
 
         lax.fori_loop(0, 16, eight, h0)
 
-    for_each(4, forward)
-
-    for ctx in (0, 1):
-        for g in range(GROUPS):
-            at = slice(g * LANES, (g + 1) * LANES)
-            rows = slice(ctx * ROWS, (ctx + 1) * ROWS)
-            zv = zz[rows, at]
-            val = (yy[rows, at] * zv * jax.nn.sigmoid(zv)).astype(BF16)
-            mid[rows, at] = val
-            mid_t[at, rows] = jnp.transpose(val.astype(F32)).astype(BF16)
-
-    gbr_copy.wait()
-
-    def out_grads(i):
-        e = pl.ds(pl.multiple_of(i * 256, 256), 256)
-        branch = gbr[...].reshape(256, 1024)
-        for half in (0, 1):
-            got = dot_nn(mid_t[e, :], branch[:, half * 512 : (half + 1) * 512])
-            go_w[half, i // 2, i % 2] = got.astype(BF16).reshape(2, 128, 512)
-
-    for_each(4, out_grads)
-    scatter_o = HalfScatter(sems, go_w, o1, o2, o3)
-    scatter_o.push1(1)
+    gbr_copy.wait_recv()
 
     def branch_back(i):
         branch = gbr[...].reshape(256, 1024)
@@ -1270,14 +1138,11 @@
         gs[:, at] = gm * (zv * sigma)
         gz[:, at] = (gm * yy[:, at] * (sigma * (1.0 + zv * (1.0 - sigma)))).astype(BF16)
 
-
     def z_grads(i):
         d = pl.ds(pl.multiple_of(i * 128, 128), 128)
         for half in (0, 1):
             got = dot_nn(nrm_t[d, :], gz[:, half * 512 : (half + 1) * 512])
             gz_w[half, i // 2, i % 2] = got.astype(BF16).reshape(2, 64, 512)
-
-    scatter_z = Scatter(sems, gz_w, z1, z2, z3)
 
     def backward_ends(q):
         ctx, block = q // 2, q % 2
@@ -1295,6 +1160,28 @@
         adj = lax.fori_loop(0, 16, eight, jnp.zeros((16, WIDE), F32))
         for g in range(4):
             lp[ctx * GROUPS + block * 4 + g] = adj[:, g * LANES : (g + 1) * LANES]
+
+    return_states.done()
+    for_each(4, forward)
+    for ctx in (0, 1):
+        for g in range(GROUPS):
+            at = slice(g * LANES, (g + 1) * LANES)
+            rows = slice(ctx * ROWS, (ctx + 1) * ROWS)
+            zv = zz[rows, at]
+            val = (yy[rows, at] * zv * jax.nn.sigmoid(zv)).astype(BF16)
+            mid[rows, at] = val
+            mid_t[at, rows] = jnp.transpose(val.astype(F32)).astype(BF16)
+
+    def out_grads(i):
+        e = pl.ds(pl.multiple_of(i * 256, 256), 256)
+        branch = gbr[...].reshape(256, 1024)
+        for half in (0, 1):
+            got = dot_nn(mid_t[e, :], branch[:, half * 512 : (half + 1) * 512])
+            go_w[half, i // 2, i % 2] = got.astype(BF16).reshape(2, 128, 512)
+
+    for_each(4, out_grads)
+    scatter_o = HalfScatter(sems, go_w, o1, o2, o3)
+    scatter_o.push1(1)
 
     for j in (0, 1):
         gather_o.slot_done(j)
@@ -1306,12 +1193,13 @@
     send_adj = Transpose(sems, lp, lpr)
     send_adj.start()
     for_each(8, z_grads)
+    scatter_z = Scatter(sems, gz_w, z1, z2, z3)
     send_adj.done()
     state = jnp.zeros((16, LANES), F32)
     for s in range(15, -1, -1):
-        hret[s] = state
+        lret[s] = state
         state = hpr[s, 1] * state + lpr[s]
-    return_adj = Transpose(sems, hret, hin)
+    return_adj = Transpose(sems, lret, lin)
     return_adj.start()
     scatter_o.push1(0)
     scatter_z.push1(2)
@@ -1322,12 +1210,6 @@
             rowx[ctx, :, half * 512 : (half + 1) * 512] = got[ctx * ROWS : (ctx + 1) * ROWS]
     rows_copy = sems.copy(rowx.at[mate], rowx_in.at[0], mate, seq)
     rows_copy.start()
-    rows_copy.wait()
-    for g in range(GROUPS):
-        at = slice(g * LANES, (g + 1) * LANES)
-        o_out[:, at] = (
-            hid[:, at].astype(F32) + live * (rowx[c, :, at] + rowx_in[0, :, at])
-        ).astype(BF16)
     return_adj.done()
 
     sub = lax.broadcasted_iota(jnp.int32, (8, LANES), 0)
@@ -1364,7 +1246,7 @@
             zz[pl.ds(t0, 8), at] = take_partial(part2)
             return adj, grad_a
 
-        adj0 = jnp.concatenate([hin[ctx * GROUPS + block * 4 + g] for g in range(4)], axis=1)
+        adj0 = jnp.concatenate([lin[ctx * GROUPS + block * 4 + g] for g in range(4)], axis=1)
         _, grad_a = lax.fori_loop(0, 16, eight, (adj0, jnp.zeros((16, WIDE), F32)))
         hs[ctx * 129, :, at] = grad_a
 
@@ -1389,14 +1271,15 @@
     backward(0, 0)
     scatter_o.push2(1)
     scatter_z.push1(1)
-    scatter_z.push1(0)
     backward(0, 1)
     scatter_o.push2(0)
+    scatter_z.push1(0)
     for_each(4, functools.partial(sum_lanes, 0))
     backward(1, 0)
+    scatter_z.push2(2)
+    backward(1, 1)
     scatter_o.push3(1)
-    backward(1, 1)
-    scatter_z.push2(2)
+    scatter_z.push2(3)
     for_each(4, functools.partial(sum_lanes, 1))
 
     ones = []
@@ -1411,13 +1294,19 @@
     total = jnp.zeros((256, 64), F32)
     for j in range(GROUPS):
         total = total + dot_nt(
-            mid[:, j * LANES : (j + 1) * LANES], wp[j // 4, (j // 2) % 2, j % 2, 96:160, :]
+            mid[:, j * LANES : (j + 1) * LANES], wp[1, j // 4, (j // 2) % 2, j % 2, 0:64, :]
         )
     xd_out[:, 0:64] = total
     xd_out[:, 64:128] = gbc[:, 64:128]
     gd_copy = sems.copy(xd_out, xd_in, mate, seq)
+    rows_copy.wait()
     gd_copy.start()
-    scatter_z.push2(3)
+    for g in range(GROUPS):
+        at = slice(g * LANES, (g + 1) * LANES)
+        o_out[:, at] = (
+            hid[:, at].astype(F32) + live * (rowx[c, :, at] + rowx_in[0, :, at])
+        ).astype(BF16)
+    scatter_z.push2(1)
     gd_copy.wait()
     g_dbl = (xd_out[...] + xd_in[...]).astype(BF16)
 
@@ -1425,7 +1314,7 @@
         for j in range(GROUPS):
             at = slice(j * LANES, (j + 1) * LANES)
             rows = slice(ctx * ROWS, (ctx + 1) * ROWS)
-            back = dot_nn(g_dbl[rows, :], wp[j // 4, (j // 2) % 2, j % 2, 0:128, :])
+            back = dot_nn(g_dbl[rows, 0:96], wp[0, j // 4, (j // 2) % 2, j % 2])
             g_sig = gs[rows, at] * prm[22:23, at] + zz[rows, at] * delta[rows, at] + back
             v = conv_rows(ctx, at)
             sigma = jax.nn.sigmoid(v)
@@ -1435,7 +1324,7 @@
     ]
     for copy in edge_copies:
         copy.start()
-    scatter_z.push2(1)
+    scatter_z.push2(0)
     scatter_o.push3(0)
 
     def small_grads():
@@ -1449,7 +1338,7 @@
             at = slice(j * LANES, (j + 1) * LANES)
             to = (j // 4, (j // 2) % 2, j % 2)
             sv = sig[:, at].astype(F32)
-            gp_w[to + (slice(0, 96),)] = dot_nn(g_t, sig[:, at]).astype(BF16)
+            gp_w[(0,) + to] = dot_nn(g_t, sig[:, at]).astype(BF16)
             g_dtw = dot_nn(low_t, mid[:, at])
             taps = []
             for k in range(4):
@@ -1469,14 +1358,14 @@
                 + [bias, g_bdt[:, at], skip, jnp.zeros((9, LANES), F32)],
                 axis=0,
             )
-            gp_w[to + (slice(96, 192),)] = rest.astype(BF16)
+            gp_w[(1,) + to] = rest.astype(BF16)
 
     small_grads()
-    scatter_p = SmallScatter(sems, gp_w, p1, p2, p3)
-    scatter_p.push1()
+    scatter_p = HalfScatter(sems, gp_w, p1, p2, p3)
+    scatter_p.all1()
 
     for copy in edge_copies:
-        copy.wait()
+        copy.wait_recv()
     last_chip = (seq < 15).astype(F32)
     for ctx in (0, 1):
         gext[ctx, 128:136, :] = gedge[ctx] * last_chip
@@ -1499,7 +1388,6 @@
             gx_w[half, i // 2, i % 2] = got.astype(BF16).reshape(2, 64, 512)
 
     scatter_x = Scatter(sems, gx_w, x1, x2, x3)
-    scatter_z.push2(0)
     for j in scatter_x.order:
         zj = partner(z, j)
         x_grads(2 * zj)
@@ -1518,12 +1406,14 @@
 
     for i in range(4):
         normed_back(i)
+    scatter_p.all2()
     scatter_x.push2(2)
     for i in range(4, 8):
         normed_back(i)
     back_copy = sems.copy(rowx.at[mate], rowx_in.at[1], mate, seq)
     back_copy.start()
     scatter_x.push2(3)
+    scatter_p.all3()
     scatter_x.push2(1)
 
     def hidden_rows(i):
@@ -1540,7 +1430,6 @@
     scatter_x.push2(0)
     scatter_x.push3(3)
     scatter_x.push3(1)
-    scatter_p.push2()
     scatter_x.push3(0)
     scatter_o.done()
     out_copy = sems.copy(o_gout, o_gout, mate, seq)
@@ -1556,12 +1445,13 @@
         fin[2 + half] = scatter_z.result(half)
     z_copy = sems.copy(fin.at[pl.ds(2, 2)], fin_in.at[pl.ds(2, 2)], mate, seq)
     z_copy.start()
-    scatter_p.push3()
+    scatter_p.done()
     small_copy = sems.copy(fsm, fsm, mate, seq)
 
     @pl.when(is_active())
     def _():
-        fsm[...] = scatter_p.result()
+        for half in (0, 1):
+            fsm[half * 96 : (half + 1) * 96, :] = scatter_p.result(half)
         small_copy.start()
 
     def weight_rows(part, gain_sum):
@@ -1577,6 +1467,10 @@
     gain_sum = weight_rows(1, jnp.zeros((64, LANES), F32))
     for group in (gather_x, gather_z, gather_o, gather_p, scatter_z, scatter_o):
         group.sent()
+    for group in (send_ends, return_states, send_adj, return_adj):
+        group.sent()
+    for copy in hid_copies + edge_copies + [gbr_copy, gain_all]:
+        copy.wait_send()
 
     scatter_x.done()
     for half in (0, 1):
@@ -1659,11 +1553,11 @@
         vmem((2, 4, 2, 2, 64, 512), BF16),
         vmem((2, 4, 2, 2, 64, 512), BF16),
         vmem((2, 2, 2, 2, 128, 512), BF16),
-        vmem((2, 2, 2, 192, LANES), BF16),
+        vmem((2, 2, 2, 2, 96, LANES), BF16),
         vmem((2, 4, 2, 2, 64, 512), BF16),
         vmem((2, 4, 2, 2, 64, 512), BF16),
         vmem((2, 2, 2, 2, 128, 512), BF16),
-        vmem((2, 2, 2, 192, LANES), BF16),
+        vmem((2, 2, 2, 2, 96, LANES), BF16),
     ]
     for z_count, rows, columns in ((4, 64, 512), (4, 64, 512), (2, 128, 512)):
         scratch += [
@@ -1672,11 +1566,13 @@
             vmem((3, 2, rows, columns), BF16),
         ]
     scratch += [
-        vmem((3, 2, 2, 192, LANES), BF16),
-        vmem((2, 192, LANES), BF16),
-        vmem((192, LANES), BF16),
+        vmem((2, 2, 2, 96, LANES), BF16),
+        vmem((2, 2, 96, LANES), BF16),
+        vmem((3, 2, 96, LANES), BF16),
         vmem((16, 2, 16, LANES), F32),
         vmem((16, 2, 16, LANES), F32),
+        vmem((16, 16, LANES), F32),
+        vmem((16, 16, LANES), F32),
         vmem((16, 16, LANES), F32),
         vmem((16, 16, LANES), F32),
         vmem((16, 16, LANES), F32),

time: 166 us -> 155 us (0.934)
  Pallas kernels: 162 us -> 151 us
    pallas_call x1, Pallas kernels: 159 us -> 148 us  [fused_shards(): pl.pallas_call(fused_kernel, out_shape=(jax.ShapeDtypeStruct((128, 1024),...]
where the time goes in v2:
time: 155 us; the launch traced here: 154 us
  Pallas kernels  151 us (97%)
    pallas_call x1, Pallas kernels, fused_shards(): pl.pallas_call(fused_kernel, out_shape=(jax.ShapeDtypeStruct((128, 1024),...  148 us
    pallas_call x1, Pallas kernels, fused_shards(): pl.pallas_call(place_outputs, out_shape=tuple((jax.ShapeDtypeStruct(shape...  3.18 us

profile of v2, /device:TPU:0, one launch (start us, length us, event | category | flops | bytes accessed | tf_op | source)
XLA Modules:
  0.0 154.4 jit_solution(14875991344761154741)
XLA Ops:
  1.3 0.0 copy-start.3
  1.3 0.6 copy-done.3
  1.9 0.0 copy-start
  1.9 0.0 copy-start.1
  2.0 0.0 copy-start.2
  2.0 0.1 maximum_bitcast_fusion
  2.0 0.6 copy-done
  2.6 0.0 copy-done.1
  2.6 0.0 copy-done.2
  2.6 0.6 maximum_convert_fusion.vectors
  3.2 148.0 %shard_map.229 = (bf16[128,1024]{1,0:T(8,128)(2,1)}, f32[128,1024]{1,0:T(8,128)}, f32[64,4096]{1,0:T(8,128)}, f32[128,1024]{1,0:T(8,128)}, f32[192,128]{1,0:T(8,128)}, /*index=5*/f32[64,128]{1,0:T(8,128)}) custom-call(s32[1]{0:T(128)S(6)} %copy.26.valid, bf16[128,1024]{1,0:T(8,128)(2,1)} %bitcast.21, bf16[128,1024]{1,0:T(8,128)(2,1)} %bitcast.22, ...), custom_call_target="tpu_custom_call" | custom-call | tf_op jit(solution)/shard_map/pallas_call | solution.py:1593
  151.3 3.2 %shard_map.230 = (bf16[128,1024]{1,0:T(8,128)(2,1)}, f32[128,1024]{1,0:T(8,128)}, f32[1,64]{1,0:T(1,128)}, f32[64,4096]{1,0:T(8,128)}, f32[4,128]{1,0:T(4,128)},...) custom-call(bf16[128,1024]{1,0:T(8,128)(2,1)} %get-tuple-element.30., ...), custom_call_target="tpu_custom_call" | custom-call | tf_op jit(solution)/shard_map/pallas_call | solution.py:1622
Async XLA Ops:
  1.3 0.7 copy-start.3
  1.9 0.7 copy-start
  1.9 0.7 copy-start.1
  2.0 0.7 copy-start.2

commit v3 on v2

--- a/solution.py
+++ b/solution.py
@@ -432,11 +432,12 @@
 class Gather:
     slots = 4
 
-    def __init__(self, sems, buf):
+    def __init__(self, sems, buf, rows):
         c, _, z, y, x = place()
+        rows = pl.ds(0, rows)
         own = self.slot(0)
         self.first = [
-            sems.copy(buf.at[:, own, y, x], buf.at[:, own, y, x], c, chip(partner(z, j), y, x))
+            sems.copy(buf.at[:, own, y, x, rows], buf.at[:, own, y, x, rows], c, chip(partner(z, j), y, x))
             for j in (1, 2, 3)
         ]
         send2, send3 = sems.new_send(), sems.new_send()
@@ -446,21 +447,21 @@
             got = sems.new_receive()
             self.second.append(
                 [
-                    sems.copy(buf.at[0, s, y, x], buf.at[0, s, y, x], c, chip(z, 1 - y, x), send2, got),
-                    sems.copy(buf.at[1, s, y, x], buf.at[1, s, y, x], c, chip(z, y, 1 - x), send2, got),
+                    sems.copy(buf.at[0, s, y, x, rows], buf.at[0, s, y, x, rows], c, chip(z, 1 - y, x), send2, got),
+                    sems.copy(buf.at[1, s, y, x, rows], buf.at[1, s, y, x, rows], c, chip(z, y, 1 - x), send2, got),
                 ]
             )
-            self.second_all.append(joint(buf.at[:, s, y, x], (send2, got)))
+            self.second_all.append(joint(buf.at[:, s, y, x, rows], (send2, got)))
             got = sems.new_receive()
             self.third.append(
                 [
-                    sems.copy(buf.at[0, s, :, x], buf.at[0, s, :, x], c, chip(z, y, 1 - x), send3, got),
-                    sems.copy(buf.at[1, s, y], buf.at[1, s, y], c, chip(z, 1 - y, x), send3, got),
+                    sems.copy(buf.at[0, s, :, x, rows], buf.at[0, s, :, x, rows], c, chip(z, y, 1 - x), send3, got),
+                    sems.copy(buf.at[1, s, y, :, rows], buf.at[1, s, y, :, rows], c, chip(z, 1 - y, x), send3, got),
                 ]
             )
-            self.third_all.append(joint(buf.at[:, s, :, x], (send3, got)))
-        self.second_sent = joint(buf.at[:, :, y, x], (send2, got))
-        self.third_sent = joint(buf.at[:, :, :, x], (send3, got))
+            self.third_all.append(joint(buf.at[:, s, :, x, rows], (send3, got)))
+        self.second_sent = joint(buf.at[:, :, y, x, rows], (send2, got))
+        self.third_sent = joint(buf.at[:, :, :, x, rows], (send3, got))
 
     def slot(self, j):
         return partner(place()[2], j)
@@ -553,8 +554,9 @@
 class Scatter:
     order = (2, 3, 1, 0)
 
-    def __init__(self, sems, grad, came1, came2, came3):
+    def __init__(self, sems, grad, came1, came2, came3, rows):
         c, _, z, y, x = place()
+        rows = self.rows = pl.ds(0, rows)
         self.grad, self.came1, self.came2, self.came3 = grad, came1, came2, came3
         send1, send2 = sems.new_send(), sems.new_send()
         self.first, self.first_all, self.second, self.second_all = [], [], [], []
@@ -563,16 +565,16 @@
             got = sems.new_receive()
             self.first.append(
                 [
-                    sems.copy(grad.at[0, s, :, 1 - x], came1.at[0, s], c, chip(z, y, 1 - x), send1, got),
-                    sems.copy(grad.at[1, s, 1 - y], came1.at[1, s], c, chip(z, 1 - y, x), send1, got),
+                    sems.copy(grad.at[0, s, :, 1 - x, rows], came1.at[0, s], c, chip(z, y, 1 - x), send1, got),
+                    sems.copy(grad.at[1, s, 1 - y, :, rows], came1.at[1, s], c, chip(z, 1 - y, x), send1, got),
                 ]
             )
             self.first_all.append(joint(came1.at[:, s], (send1, got)))
             got = sems.new_receive()
             self.second.append(
                 [
-                    sems.copy(grad.at[0, s, 1 - y, x], came2.at[0, s], c, chip(z, 1 - y, x), send2, got),
-                    sems.copy(grad.at[1, s, y, 1 - x], came2.at[1, s], c, chip(z, y, 1 - x), send2, got),
+                    sems.copy(grad.at[0, s, 1 - y, x, rows], came2.at[0, s], c, chip(z, 1 - y, x), send2, got),
+                    sems.copy(grad.at[1, s, y, 1 - x, rows], came2.at[1, s], c, chip(z, y, 1 - x), send2, got),
                 ]
             )
             self.second_all.append(joint(came2.at[:, s], (send2, got)))
@@ -581,7 +583,7 @@
         got = sems.new_receive()
         self.third = [
             sems.copy(
-                grad.at[:, self.slot(self.third_slot(j)), y, x],
+                grad.at[:, self.slot(self.third_slot(j)), y, x, rows],
                 came3.at[j - 1],
                 c,
                 chip(partner(z, j), y, x),
@@ -606,19 +608,19 @@
         _, _, _, y, x = place()
         s = self.slot(j)
         self.first_all[j].wait_recv()
-        add_into(self.grad.at[0, s, 1 - y, x], self.came1.at[0, s, 1 - y])
+        add_into(self.grad.at[0, s, 1 - y, x, self.rows], self.came1.at[0, s, 1 - y])
         self.second[j][0].start()
-        add_into(self.grad.at[1, s, y, 1 - x], self.came1.at[1, s, 1 - x])
+        add_into(self.grad.at[1, s, y, 1 - x, self.rows], self.came1.at[1, s, 1 - x])
         self.second[j][1].start()
-        add_into(self.grad.at[0, s, y, x], self.came1.at[0, s, y])
-        add_into(self.grad.at[1, s, y, x], self.came1.at[1, s, x])
+        add_into(self.grad.at[0, s, y, x, self.rows], self.came1.at[0, s, y])
+        add_into(self.grad.at[1, s, y, x, self.rows], self.came1.at[1, s, x])
 
     def push3(self, j):
         _, _, _, y, x = place()
         s = self.slot(j)
         self.second_all[j].wait_recv()
         for half in (0, 1):
-            add_into(self.grad.at[half, s, y, x], self.came2.at[half, s])
+            add_into(self.grad.at[half, s, y, x, self.rows], self.came2.at[half, s])
         self.send_on(j)
 
     def send_on(self, j):
@@ -651,7 +653,7 @@
 
     def result(self, half):
         _, _, _, y, x = place()
-        total = self.grad[half, self.slot(0), y, x].astype(F32)
+        total = self.grad[half, self.slot(0), y, x, self.rows].astype(F32)
         for k in range(3):
             total = total + self.came3[k, half].astype(F32)
         return total
@@ -693,6 +695,99 @@
             self.third[2].wait_send()
 
         self.sent_rest()
+
+
+class AcrossGather:
+    def __init__(self, sems, buf, first, count):
+        c, _, z, y, x = place()
+        rows = pl.ds(first, count)
+        self.first = sems.copy(
+            buf.at[:, z, y, x, rows], buf.at[:, z, y, x, rows], c, chip(z, y, 1 - x)
+        )
+        self.second = sems.copy(
+            buf.at[:, z, y, :, rows], buf.at[:, z, y, :, rows], c, chip(z, 1 - y, x)
+        )
+        self.third = [
+            sems.copy(
+                buf.at[:, z, :, :, rows], buf.at[:, z, :, :, rows], c, chip(partner(z, j), y, x)
+            )
+            for j in (1, 2, 3)
+        ]
+
+    def start(self):
+        self.first.start()
+
+    def relay(self):
+        self.first.wait_recv()
+        self.second.start()
+
+    def cross(self):
+        self.second.wait_recv()
+        for copy in self.third:
+            copy.start()
+
+    def done(self):
+        for copy in self.third:
+            copy.wait_recv()
+
+    def sent(self):
+        for copy in [self.first, self.second] + self.third:
+            copy.wait_send()
+
+
+class AcrossScatter:
+    def __init__(self, sems, grad, came1, came2, came3, first, count):
+        c, _, z, y, x = place()
+        rows = self.rows = pl.ds(first, count)
+        self.grad, self.came1, self.came2, self.came3 = grad, came1, came2, came3
+        got = sems.new_receive()
+        self.first = [
+            sems.copy(
+                grad.at[:, partner(z, j), :, :, rows],
+                came1.at[j - 1],
+                c,
+                chip(partner(z, j), y, x),
+                None,
+                got,
+            )
+            for j in (1, 2, 3)
+        ]
+        self.first_all = joint(came1, (sems.new_send(), got))
+        self.second = sems.copy(grad.at[:, z, 1 - y, :, rows], came2, c, chip(z, 1 - y, x))
+        self.third = sems.copy(grad.at[:, z, y, 1 - x, rows], came3, c, chip(z, y, 1 - x))
+
+    def push1(self):
+        for copy in self.first:
+            copy.start()
+
+    def push2(self):
+        _, _, z, y, _ = place()
+        self.first_all.wait_recv()
+        for row in (1 - y, y):
+            for half in (0, 1):
+                total = self.grad[half, z, row, :, self.rows].astype(F32)
+                for k in range(3):
+                    total = total + self.came1[k, half, row].astype(F32)
+                self.grad[half, z, row, :, self.rows] = total.astype(BF16)
+        self.second.start()
+
+    def push3(self):
+        _, _, z, y, _ = place()
+        self.second.wait_recv()
+        for half in (0, 1):
+            add_into(self.grad.at[half, z, y, :, self.rows], self.came2.at[half])
+        self.third.start()
+
+    def done(self):
+        self.third.wait_recv()
+
+    def result(self, half):
+        _, _, z, y, x = place()
+        return self.grad[half, z, y, x, self.rows].astype(F32) + self.came3[half].astype(F32)
+
+    def sent(self):
+        for copy in self.first + [self.second, self.third]:
+            copy.wait_send()
 
 
 class Transpose:
@@ -780,11 +875,11 @@
 
 def fused_kernel(
     valid,
-    hid,
-    out_g,
+    hid_hbm,
+    out_g_hbm,
     resets,
-    in_w,
-    out_w,
+    in_w_hbm,
+    out_w_hbm,
     x_w,
     dt_w,
     a_log,
@@ -843,6 +938,9 @@
     p1,
     p2,
     p3,
+    c1,
+    c2,
+    c3,
     hp,
     hpr,
     hret,
@@ -860,6 +958,9 @@
     fin,
     fin_in,
     fsm,
+    in_w,
+    out_g,
+    load_sems,
     send_sems,
     recv_sems,
 ):
@@ -878,16 +979,40 @@
     pl.semaphore_signal(barrier, inc=1, device_id=(mate, after), device_id_type=MESH)
     pl.semaphore_signal(barrier, inc=1, device_id=(mate, before), device_id_type=MESH)
 
+    hid = hidb.at[c, pl.ds(16, ROWS), :]
+    loads = [
+        pltpu.make_async_copy(hid_hbm, hid, load_sems.at[0]),
+        pltpu.make_async_copy(out_g_hbm, out_g, load_sems.at[1]),
+    ]
     for half in (0, 1):
-        wx[half, z, y, x] = in_w[:, pl.ds(pl.multiple_of(c * 1024 + half * 512, 512), 512)]
-        wz[half, z, y, x] = in_w[
-            :, pl.ds(pl.multiple_of(2048 + c * 1024 + half * 512, 512), 512)
-        ]
+        for part, ref in ((0, wx), (1, wz)):
+            at = pl.ds(pl.multiple_of(part * 2048 + c * 1024 + half * 512, 512), 512)
+            loads.append(
+                pltpu.make_async_copy(
+                    in_w_hbm.at[:, at], ref.at[half, z, y, x], load_sems.at[2 + 2 * half + part]
+                )
+            )
+    out_loads = [
+        pltpu.make_async_copy(
+            out_w_hbm.at[:, pl.ds(half * 512, 512)],
+            wo.at[half, z % 2, y, x],
+            load_sems.at[6 + half],
+        )
+        for half in (0, 1)
+    ]
+    in_load = pltpu.make_async_copy(in_w_hbm, in_w, load_sems.at[8])
+    for load in loads:
+        load.start()
+
+    @pl.when(is_active())
+    def _():
+        for load in out_loads:
+            load.start()
+
+    in_load.start()
 
     @pl.when(z // 2 == c)
     def _():
-        for half in (0, 1):
-            wo[half, z % 2, y, x] = out_w[:, half * 512 : (half + 1) * 512]
         wp[0, z % 2, y, x] = x_w[...]
         wp[1, z % 2, y, x, 0:64, :] = dt_w[...]
         wp[1, z % 2, y, x, 64:80, :] = a_log[...]
@@ -903,17 +1028,28 @@
     )
     row_place = seq * ROWS + lax.broadcasted_iota(jnp.int32, (ROWS, LANES), 0)
     live = (row_place < valid[0]).astype(F32)
-    hidb[c, pl.ds(16, ROWS), :] = hid[...]
+    loads[1].wait()
     for g in range(GROUPS):
         at = slice(g * LANES, (g + 1) * LANES)
         gbr[c, :, at] = (live * out_g[:, at].astype(F32)).astype(BF16)
 
+    loads[0].wait()
+    for load in loads[2:]:
+        load.wait()
+
+    @pl.when(is_active())
+    def _():
+        for load in out_loads:
+            load.wait()
+
+    in_load.wait()
     pl.semaphore_wait(barrier, 18)
 
-    gather_x = Gather(sems, wx)
-    gather_z = Gather(sems, wz)
-    gather_o = HalfGather(sems, wo)
-    gather_p = HalfGather(sems, wp)
+    gather_x = Gather(sems, wx, 64)
+    gather_z = Gather(sems, wz, 48)
+    across_z = AcrossGather(sems, wz, 48, 16)
+    gather_o = HalfGather(sems, wo, 128)
+    gather_p = HalfGather(sems, wp, 96)
     gain_sems = (sems.new_send(), sems.new_receive())
     gain_copies = [
         sems.copy(gain_b.at[seq], gain_b.at[seq], c, (seq + k) % 16, *gain_sems)
@@ -931,6 +1067,7 @@
         copy.start()
     for copy in gain_copies:
         copy.start()
+    across_z.start()
     gather_p.start()
     gather_x.start()
     gather_x.relay(0)
@@ -955,6 +1092,7 @@
     gather_p.cross(0)
     gather_p.cross(1)
     gather_z.start()
+    across_z.relay()
     for ctx in (0, 1):
         for g in range(GROUPS):
             at = slice(g * LANES, (g + 1) * LANES)
@@ -968,6 +1106,7 @@
     gather_x.cross(1)
     gather_x.relay(3)
     gather_o.start()
+    across_z.cross()
     gather_x.cross(2)
     gather_x.cross(3)
     gbr_copy.start()
@@ -1081,7 +1220,6 @@
     send_ends.start()
     gather_o.relay(0)
     gather_o.relay(1)
-    gather_z.done()
 
     def z_columns(i):
         rows = nrm_rows()
@@ -1093,7 +1231,6 @@
     def nrm_rows():
         return jnp.concatenate([nrm[0, 16:144, :], nrm[1, 16:144, :]], axis=0)
 
-    for_each(2, z_columns)
     send_ends.done()
     state = jnp.zeros((16, LANES), F32)
     for s in range(16):
@@ -1103,6 +1240,9 @@
     return_states.start()
     gather_o.cross(0)
     gather_o.cross(1)
+    gather_z.done()
+    across_z.done()
+    for_each(2, z_columns)
 
     def forward(q):
         ctx, block = q // 2, q % 2
@@ -1180,7 +1320,7 @@
             go_w[half, i // 2, i % 2] = got.astype(BF16).reshape(2, 128, 512)
 
     for_each(4, out_grads)
-    scatter_o = HalfScatter(sems, go_w, o1, o2, o3)
+    scatter_o = HalfScatter(sems, go_w, o1, o2, o3, 128)
     scatter_o.push1(1)
 
     for j in (0, 1):
@@ -1193,7 +1333,8 @@
     send_adj = Transpose(sems, lp, lpr)
     send_adj.start()
     for_each(8, z_grads)
-    scatter_z = Scatter(sems, gz_w, z1, z2, z3)
+    scatter_z = Scatter(sems, gz_w, z1, z2, z3, 48)
+    across_gz = AcrossScatter(sems, gz_w, c1, c2, c3, 48, 16)
     send_adj.done()
     state = jnp.zeros((16, LANES), F32)
     for s in range(15, -1, -1):
@@ -1202,6 +1343,7 @@
     return_adj = Transpose(sems, lret, lin)
     return_adj.start()
     scatter_o.push1(0)
+    across_gz.push1()
     scatter_z.push1(2)
     scatter_z.push1(3)
     for half in (0, 1):
@@ -1276,6 +1418,7 @@
     scatter_z.push1(0)
     for_each(4, functools.partial(sum_lanes, 0))
     backward(1, 0)
+    across_gz.push2()
     scatter_z.push2(2)
     backward(1, 1)
     scatter_o.push3(1)
@@ -1301,10 +1444,11 @@
     gd_copy = sems.copy(xd_out, xd_in, mate, seq)
     rows_copy.wait()
     gd_copy.start()
+    across_gz.push3()
     for g in range(GROUPS):
         at = slice(g * LANES, (g + 1) * LANES)
         o_out[:, at] = (
-            hid[:, at].astype(F32) + live * (rowx[c, :, at] + rowx_in[0, :, at])
+            hidb[c, 16:144, at].astype(F32) + live * (rowx[c, :, at] + rowx_in[0, :, at])
         ).astype(BF16)
     scatter_z.push2(1)
     gd_copy.wait()
@@ -1361,7 +1505,7 @@
             gp_w[(1,) + to] = rest.astype(BF16)
 
     small_grads()
-    scatter_p = HalfScatter(sems, gp_w, p1, p2, p3)
+    scatter_p = HalfScatter(sems, gp_w, p1, p2, p3, 96)
     scatter_p.all1()
 
     for copy in edge_copies:
@@ -1387,7 +1531,7 @@
             got = dot_nn(nrm_t[d, :], mid[:, half * 512 : (half + 1) * 512])
             gx_w[half, i // 2, i % 2] = got.astype(BF16).reshape(2, 64, 512)
 
-    scatter_x = Scatter(sems, gx_w, x1, x2, x3)
+    scatter_x = Scatter(sems, gx_w, x1, x2, x3, 64)
     for j in scatter_x.order:
         zj = partner(z, j)
         x_grads(2 * zj)
@@ -1418,7 +1562,7 @@
 
     def hidden_rows(i):
         at = pl.ds(pl.multiple_of(i * 16, 16), 16)
-        rows = hid[at, :].astype(F32)
+        rows = hidb[c, pl.ds(pl.multiple_of(16 + i * 16, 16), 16), :].astype(F32)
         r = lax.rsqrt(jnp.mean(rows * rows, axis=1, keepdims=True) + epsilon)
         g_hat = (rowx[c, at, :] + rowx_in[1, at, :]) * gain_row
         inner = jnp.mean(g_hat * rows, axis=1, keepdims=True)
@@ -1441,8 +1585,10 @@
         out_copy.start()
 
     scatter_z.done()
+    across_gz.done()
     for half in (0, 1):
-        fin[2 + half] = scatter_z.result(half)
+        fin[2 + half, 0:48, :] = scatter_z.result(half)
+        fin[2 + half, 48:64, :] = across_gz.result(half)
     z_copy = sems.copy(fin.at[pl.ds(2, 2)], fin_in.at[pl.ds(2, 2)], mate, seq)
     z_copy.start()
     scatter_p.done()
@@ -1467,7 +1613,7 @@
     gain_sum = weight_rows(1, jnp.zeros((64, LANES), F32))
     for group in (gather_x, gather_z, gather_o, gather_p, scatter_z, scatter_o):
         group.sent()
-    for group in (send_ends, return_states, send_adj, return_adj):
+    for group in (across_z, across_gz, send_ends, return_states, send_adj, return_adj):
         group.sent()
     for copy in hid_copies + edge_copies + [gbr_copy, gain_all]:
         copy.wait_send()
@@ -1521,7 +1667,7 @@
         ]
     )
     vmem = pltpu.VMEM
-    count = 88
+    sends, receives = 71, 92
     scratch = [
         vmem((2, 144, 1024), BF16),
         vmem((2, 128, 1024), BF16),
@@ -1559,7 +1705,7 @@
         vmem((2, 2, 2, 2, 128, 512), BF16),
         vmem((2, 2, 2, 2, 96, LANES), BF16),
     ]
-    for z_count, rows, columns in ((4, 64, 512), (4, 64, 512), (2, 128, 512)):
+    for z_count, rows, columns in ((4, 64, 512), (4, 48, 512), (2, 128, 512)):
         scratch += [
             vmem((2, z_count, 2, rows, columns), BF16),
             vmem((2, z_count, rows, columns), BF16),
@@ -1569,6 +1715,9 @@
         vmem((2, 2, 2, 96, LANES), BF16),
         vmem((2, 2, 96, LANES), BF16),
         vmem((3, 2, 96, LANES), BF16),
+        vmem((3, 2, 2, 2, 16, 512), BF16),
+        vmem((2, 2, 16, 512), BF16),
+        vmem((2, 16, 512), BF16),
         vmem((16, 2, 16, LANES), F32),
         vmem((16, 2, 16, LANES), F32),
         vmem((16, 16, LANES), F32),
@@ -1586,10 +1735,14 @@
         vmem((4, 64, 512), F32),
         vmem((4, 64, 512), F32),
         vmem((192, LANES), F32),
-        pltpu.SemaphoreType.DMA((count,)),
-        pltpu.SemaphoreType.DMA((count,)),
+        vmem((64, 4096), BF16),
+        vmem((128, 1024), BF16),
+        pltpu.SemaphoreType.DMA((9,)),
+        pltpu.SemaphoreType.DMA((sends,)),
+        pltpu.SemaphoreType.DMA((receives,)),
     ]
     whole = pl.BlockSpec(memory_space=pltpu.VMEM)
+    hbm = pl.BlockSpec(memory_space=pl.ANY)
     parts = pl.pallas_call(
         fused_kernel,
         out_shape=(
@@ -1600,7 +1753,7 @@
             jax.ShapeDtypeStruct((192, LANES), F32),
             jax.ShapeDtypeStruct((64, LANES), F32),
         ),
-        in_specs=[pl.BlockSpec(memory_space=pltpu.SMEM)] + [whole] * 10,
+        in_specs=[pl.BlockSpec(memory_space=pltpu.SMEM), hbm, hbm, whole, hbm, hbm] + [whole] * 5,
         out_specs=(whole,) * 6,
         scratch_shapes=scratch,
         compiler_params=pltpu.CompilerParams(

time: 155 us -> 152 us (0.981)
  Pallas kernels: 151 us -> 148 us
    pallas_call x1, Pallas kernels: 148 us -> 145 us  [fused_shards(): pl.pallas_call(fused_kernel, out_shape=(jax.ShapeDtypeStruct((128, 1024),...]
where the time goes in v3:
time: 152 us
  Pallas kernels  148 us (97%)
    pallas_call x1, Pallas kernels, fused_shards(): pl.pallas_call(fused_kernel, out_shape=(jax.ShapeDtypeStruct((128, 1024),...  145 us
    pallas_call x1, Pallas kernels, fused_shards(): pl.pallas_call(place_outputs, out_shape=tuple((jax.ShapeDtypeStruct(shape...  3.18 us

profile of v3, /device:TPU:0, one launch (start us, length us, event | category | flops | bytes accessed | tf_op | source)
XLA Modules:
  0.0 151.5 jit_solution(17699555753385537328)
XLA Ops:
  1.3 0.0 copy-start.3
  1.3 0.6 copy-done.3
  1.9 0.0 copy-start
  1.9 0.0 copy-start.1
  2.0 0.0 copy-start.2
  2.0 0.1 maximum_bitcast_fusion
  2.0 0.6 copy-done
  2.6 0.0 copy-done.1
  2.6 0.0 copy-done.2
  2.6 0.6 maximum_convert_fusion.vectors
  3.2 145.1 %shard_map.229 = (bf16[128,1024]{1,0:T(8,128)(2,1)}, f32[128,1024]{1,0:T(8,128)}, f32[64,4096]{1,0:T(8,128)}, f32[128,1024]{1,0:T(8,128)}, f32[192,128]{1,0:T(8,128)}, /*index=5*/f32[64,128]{1,0:T(8,128)}) custom-call(s32[1]{0:T(128)S(6)} %copy.26.valid, bf16[128,1024]{1,0:T(8,128)(2,1)} %bitcast.21, bf16[128,1024]{1,0:T(8,128)(2,1)} %bitcast.22, ...), custom_call_target="tpu_custom_call" | custom-call | tf_op jit(solution)/shard_map/pallas_call | solution.py:1746
  148.4 3.2 %shard_map.230 = (bf16[128,1024]{1,0:T(8,128)(2,1)}, f32[128,1024]{1,0:T(8,128)}, f32[1,64]{1,0:T(1,128)}, f32[64,4096]{1,0:T(8,128)}, f32[4,128]{1,0:T(4,128)},...) custom-call(bf16[128,1024]{1,0:T(8,128)(2,1)} %get-tuple-element.30., ...), custom_call_target="tpu_custom_call" | custom-call | tf_op jit(solution)/shard_map/pallas_call | solution.py:1775
Async XLA Ops:
  1.3 0.7 copy-start.3
  1.9 0.7 copy-start
  1.9 0.7 copy-start.1
  2.0 0.7 copy-start.2

commit v4 on v3

--- a/solution.py
+++ b/solution.py
@@ -1173,7 +1173,11 @@
     for j in range(GROUPS):
         at = slice(j * LANES, (j + 1) * LANES)
         pre = dot_nn(low[...], wp[1, j // 4, (j // 2) % 2, j % 2, 0:64, :]) + prm[21:22, at]
-        delta[:, at] = jnp.maximum(pre, 0.0) + jnp.log1p(jnp.exp(-jnp.abs(pre)))
+        decay_of = jnp.exp(-jnp.abs(pre))
+        small_log = decay_of * (1.0 - decay_of * (0.5 - decay_of * (1.0 / 3.0)))
+        delta[:, at] = jnp.maximum(pre, 0.0) + jnp.where(
+            decay_of < 0.01, small_log, jnp.log1p(decay_of)
+        )
 
     gather_z.cross(3)
 
@@ -1429,7 +1433,10 @@
     for j in range(GROUPS):
         at = slice(j * LANES, (j + 1) * LANES)
         sv = sig[:, at].astype(F32)
-        g_pre = ((yy[:, at] + zz[:, at] * sv) * (1.0 - jnp.exp(-delta[:, at]))).astype(BF16)
+        step = delta[:, at]
+        small_sigmoid = step * (1.0 - step * (0.5 - step * (1.0 / 6.0 - step * (1.0 / 24.0))))
+        sigma = jnp.where(step < 0.125, small_sigmoid, 1.0 - jnp.exp(-step))
+        g_pre = ((yy[:, at] + zz[:, at] * sv) * sigma).astype(BF16)
         mid[:, at] = g_pre
         ones.append(jnp.sum(g_pre.astype(F32), axis=0, keepdims=True))
     g_bdt = jnp.concatenate(ones, axis=1)

time: 152 us -> 152 us (level)
  no operation moved by 1% of the time
where the time goes in v4:
time: 152 us
  Pallas kernels  149 us (98%)
    pallas_call x1, Pallas kernels, fused_shards(): pl.pallas_call(fused_kernel, out_shape=(jax.ShapeDtypeStruct((128, 1024),...  145 us
    pallas_call x1, Pallas kernels, fused_shards(): pl.pallas_call(place_outputs, out_shape=tuple((jax.ShapeDtypeStruct(shape...  3.18 us

profile of v4, /device:TPU:0, one launch (start us, length us, event | category | flops | bytes accessed | tf_op | source)
XLA Modules:
  0.0 151.8 jit_solution(586838098818681315)
XLA Ops:
  1.3 0.0 copy-start.3
  1.3 0.6 copy-done.3
  1.9 0.0 copy-start
  1.9 0.0 copy-start.1
  2.0 0.0 copy-start.2
  2.0 0.1 maximum_bitcast_fusion
  2.0 0.6 copy-done
  2.6 0.0 copy-done.1
  2.6 0.0 copy-done.2
  2.6 0.6 maximum_convert_fusion.vectors
  3.2 145.4 %shard_map.229 = (bf16[128,1024]{1,0:T(8,128)(2,1)}, f32[128,1024]{1,0:T(8,128)}, f32[64,4096]{1,0:T(8,128)}, f32[128,1024]{1,0:T(8,128)}, f32[192,128]{1,0:T(8,128)}, /*index=5*/f32[64,128]{1,0:T(8,128)}) custom-call(s32[1]{0:T(128)S(6)} %copy.26.valid, bf16[128,1024]{1,0:T(8,128)(2,1)} %bitcast.21, bf16[128,1024]{1,0:T(8,128)(2,1)} %bitcast.22, ...), custom_call_target="tpu_custom_call" | custom-call | tf_op jit(solution)/shard_map/pallas_call | solution.py:1753
  148.6 3.2 %shard_map.230 = (bf16[128,1024]{1,0:T(8,128)(2,1)}, f32[128,1024]{1,0:T(8,128)}, f32[1,64]{1,0:T(1,128)}, f32[64,4096]{1,0:T(8,128)}, f32[4,128]{1,0:T(4,128)},...) custom-call(bf16[128,1024]{1,0:T(8,128)(2,1)} %get-tuple-element.30., ...), custom_call_target="tpu_custom_call" | custom-call | tf_op jit(solution)/shard_map/pallas_call | solution.py:1782
Async XLA Ops:
  1.3 0.7 copy-start.3
  1.9 0.7 copy-start
  1.9 0.7 copy-start.1
  2.0 0.7 copy-start.2
